TPU v7x, 128 devices: a whole 4x4x4 slice. The times are simulated.
128 devices in a mesh: tm: 16 (over y, x_lo, core), space: 8 (over z, x_hi).
Axes of the slice: x: 4 (x_hi: 2, x_lo: 2; x = x_hi * 2 + x_lo), y: 4, z: 4, core: 2. Of those that a mesh axis runs over, the one named last changes fastest.
Arguments:
- latents: bfloat16 [256, 64, 128, 128], P(None, 'tm', 'space'), may hold values from -6 to 6
- time_taps: bfloat16 [256, 64], P('tm'), may hold values from -2 to 2
- space_taps: float32 [256, 128, 128], P('tm'), may hold values from -1 to 1
- skip_gain: float32 [256], replicated, may hold values from 0.5 to 1.5
Outputs:
- filtered_video: bfloat16 [256, 64, 128, 128], P(None, 'tm', 'space')
All inputs are finite; a program needn't handle non-finite values.
Results may differ from a plain program's by a relative error of at most 0.007.
Values may be sent and summed in bfloat16 or wider, within the bound.
No kernel may reach another device: no remote copies, remote signals or barrier semaphores. Data moves between devices by JAX's collectives and lax.ppermute only.
A program may use at most 128 MiB of HBM per device.

v0:
```python
import math

import jax
import jax.numpy as jnp
from jax import lax
from jax.sharding import PartitionSpec as P


def dft_tables(length):
    positions = jnp.arange(length, dtype=jnp.int32)
    product = positions[:, None] * positions[None, :] % length
    angles = product.astype(jnp.float32) * (2.0 * math.pi / length)
    return (jnp.cos(angles), jnp.sin(angles))


def causal_matrix(taps):
    frames = taps.shape[1]
    target = jnp.arange(frames, dtype=jnp.int32)[:, None]
    source = jnp.arange(frames, dtype=jnp.int32)[None, :]
    offset = target - source
    picked = jnp.take(taps, jnp.maximum(offset, 0), axis=1)
    return jnp.where(offset[None] >= 0, picked, jnp.zeros_like(picked))


def convolve_time(matrix, column_piece):
    summed = jnp.einsum("nts,nshw->nthw", matrix, column_piece, preferred_element_type=jnp.float32)
    return summed.astype(jnp.bfloat16)


def rotate(operand, col_count):
    return jnp.concatenate([operand[..., col_count:], -operand[..., :col_count]], axis=-1)


def spatial_filter(frames, kernels):
    row_count = frames.shape[2]
    col_count = frames.shape[3]
    cos_rows, sin_rows = dft_tables(row_count)
    cos_cols, sin_cols = dft_tables(col_count)
    forward_cols = jnp.concatenate([cos_cols, -sin_cols], axis=1)
    forward_high = forward_cols.astype(jnp.bfloat16)
    forward_low = (forward_cols - forward_high.astype(jnp.float32)).astype(jnp.bfloat16)
    inverse_cols = jnp.concatenate([cos_cols, -sin_cols], axis=0) / float(row_count * col_count)
    three_pass = lax.Precision.HIGH

    def row_section(dft_table, operand):
        return jnp.einsum("ah,mhk->mak", dft_table, operand, precision=three_pass)

    def rows_of(col_spec):
        return row_section(cos_rows, col_spec) + rotate(row_section(sin_rows, col_spec), col_count)

    def frame_spectrum(operand):
        col_spec = jnp.einsum(
            "mhw,wk->mhk", operand, forward_high, preferred_element_type=jnp.float32
        )
        col_spec = col_spec + jnp.einsum(
            "mhw,wk->mhk", operand, forward_low, preferred_element_type=jnp.float32
        )
        return rows_of(col_spec)

    def kernel_spectrum(operand):
        col_spec = jnp.einsum("mhw,wk->mhk", operand, forward_cols, precision=three_pass)
        return rows_of(col_spec)

    def one_channel(pair_item):
        channel_frames, kernel = pair_item
        kernel_spec = kernel_spectrum(kernel[None])[0]
        kernel_re = kernel_spec[:, :col_count]
        kernel_im = kernel_spec[:, col_count:]
        frame_spec = frame_spectrum(channel_frames)
        frame_re = frame_spec[..., :col_count]
        frame_im = frame_spec[..., col_count:]
        product = jnp.concatenate(
            [
                kernel_re * frame_re - kernel_im * frame_im,
                kernel_re * frame_im + kernel_im * frame_re,
            ],
            axis=-1,
        )
        restored = row_section(cos_rows, product) - rotate(
            row_section(sin_rows, product), col_count
        )
        result = jnp.einsum("mak,kw->maw", restored, inverse_cols, precision=three_pass)
        return result.astype(jnp.bfloat16)

    return lax.map(one_channel, (frames, kernels))


def final_layout(rows_back):
    return lax.all_to_all(rows_back, "tm", split_axis=1, concat_axis=0, tiled=True)


def run_block(channel_block, time_part, space_part):
    matrix = causal_matrix(time_part)
    convolved = convolve_time(
        matrix, lax.all_to_all(channel_block, "tm", split_axis=0, concat_axis=1, tiled=True)
    )
    frames = lax.all_to_all(convolved, "space", split_axis=1, concat_axis=2, tiled=True)
    filtered = spatial_filter(frames, space_part)
    rows_back = lax.all_to_all(filtered, "space", split_axis=2, concat_axis=1, tiled=True)
    return final_layout(rows_back)


def local(latents, time_taps, space_taps, skip_gain):
    groups = lax.axis_size("tm")
    batch_count = 1
    per_group = latents.shape[0] // (groups * batch_count)
    trailing = latents.shape[1:]
    split_video = latents.reshape((groups, batch_count, per_group) + trailing)
    split_time = time_taps.reshape((batch_count, per_group) + time_taps.shape[1:])
    split_space = space_taps.reshape((batch_count, per_group) + space_taps.shape[1:])
    channel_block = split_video[:, 0].reshape((groups * per_group,) + trailing)
    result_block = run_block(channel_block, split_time[0], split_space[0])
    outputs = [result_block.reshape((groups, per_group) + trailing)]
    filtered = jnp.stack(outputs, axis=1).reshape(latents.shape)
    pre_activation = filtered.astype(jnp.float32) + skip_gain[:, None, None, None] * latents.astype(
        jnp.float32
    )
    return jax.nn.gelu(pre_activation, approximate=False).astype(jnp.bfloat16)


def solution(mesh):
    in_specs = (P(None, "tm", "space", None), P("tm", None), P("tm", None, None), P())
    out_specs = P(None, "tm", "space", None)
    return jax.shard_map(local, mesh=mesh, in_specs=in_specs, out_specs=out_specs, check_vma=False)
```

profile of v0, /device:TPU:1, one launch (start us, length us, event | category | flops | bytes accessed | tf_op | source)
XLA Modules:
  0.0 438.6 jit_solution(14309265142136979434)
XLA Ops:
  0.0 7.0 %all-to-all-start = ((bf16[256,4,16,128]{3,2,1,0:T(8,128)(2,1)}), bf16[256,4,16,128]{3,2,1,0:T(8,128)(2,1)}, u32[]{:S(2)}, u32[]{:S(2)}) async-start(bf16[256,4,16,128]{3,2,1,0:T(8,128)(2,1)} %param.6), calls=%async_computation | async-start | bytes 8388608 | tf_op jit(solution)/shard_map/all_to_all | solution.py:95
  7.2 12.1 %gather_fusion = bf16[4096,16]{1,0:T(8,128)(2,1)S(1)} fusion(bf16[16,64]{0,1:T(8,128)(2,1)S(1)} %copy.31, s32[4096]{0:T(1024)S(1)} %broadcast_clamp_fusion), kind=kCustom, calls=%fused_computation | custom fusion | bytes 278528 | tf_op jit(solution)/shard_map/jit(_take)/gather | solution.py:21
  20.0 36.8 %all-to-all-done = bf16[256,4,16,128]{3,2,1,0:T(8,128)(2,1)} async-done(((bf16[256,4,16,128]{3,2,1,0:T(8,128)(2,1)}), bf16[256,4,16,128]{3,2,1,0:T(8,128)(2,1)}, u32[]{:S(2)}, u32[]{:S(2)}) %all-to-all-start) | async-done | bytes 4194336 | tf_op jit(solution)/shard_map/all_to_all | solution.py:95
  56.7 4.5 %copy.33 = bf16[16,16,4,16,128]{4,2,0,3,1:T(4,128)(2,1)S(1)} copy(bf16[16,16,4,16,128]{4,3,2,1,0:T(8,128)(2,1)} %bitcast.4) | data formatting | bytes 8388608 | tf_op jit(solution)/shard_map/all_to_all | solution.py:95
  61.2 1.2 convolution_convert_fusion.1
  62.5 4.7 %copy.34 = bf16[16,64,16,128]{3,2,0,1:T(8,128)(2,1)} copy(bf16[16,64,16,128]{3,1,2,0:T(8,128)(2,1)S(1)} %convolution_convert_fusion.1) | data formatting | bytes 8388608 | tf_op jit(solution)/shard_map/convert_element_type | solution.py:27
  67.1 7.2 %all-to-all-start.1 = ((bf16[16,64,16,128]{3,2,0,1:T(8,128)(2,1)}), bf16[16,64,16,128]{3,2,0,1:T(8,128)(2,1)}, u32[]{:S(2)}, u32[]{:S(2)}) async-start(bf16[16,64,16,128]{3,2,0,1:T(8,128)(2,1)} %copy.34), calls=%async_computation.1 | async-start | bytes 8388608 | tf_op jit(solution)/shard_map/all_to_all | solution.py:97
  74.7 49.6 %all-to-all-done.1 = bf16[16,64,16,128]{3,2,0,1:T(8,128)(2,1)} async-done(((bf16[16,64,16,128]{3,2,0,1:T(8,128)(2,1)}), bf16[16,64,16,128]{3,2,0,1:T(8,128)(2,1)}, u32[]{:S(2)}, u32[]{:S(2)}) %all-to-all-start.1) | async-done | bytes 4194336 | tf_op jit(solution)/shard_map/all_to_all | solution.py:97
  124.2 5.4 %copy.35 = bf16[16,8,8,16,128]{4,3,2,1,0:T(8,128)(2,1)} copy(bf16[16,8,8,16,128]{4,3,0,1,2:T(8,128)(2,1)} %bitcast.8) | data formatting | bytes 8388608 | tf_op jit(solution)/shard_map/all_to_all | solution.py:97
  129.6 169.8 %while.12 = (s32[]{:T(128)}, bf16[16,8,128,128]{3,1,0,2:T(8,128)(2,1)}, f32[16,128,128]{2,1,0:T(8,128)}, f32[128,256]{1,0:T(8,128)S(1)}, bf16[16,8,128,128]{3,2,...) while((s32[]{:T(128)}, ...), condition=%wide.region_1.2_spmd.clone.clone, body=%wide.region_0.1_spmd.clone.clone.sunk | while | flops 1220820992 | bytes 24182900 | solution.py:85
  131.7 1.2 fusion.152
  132.9 1.2 convolution_add_fusion.2
  134.1 1.1 convolution_bitcast_fusion.9
  142.3 1.2 fusion.152
  143.5 1.2 convolution_add_fusion.2
  144.7 1.1 convolution_bitcast_fusion.9
  152.9 1.2 fusion.152
  154.1 1.2 convolution_add_fusion.2
  155.3 1.1 convolution_bitcast_fusion.9
  163.5 1.2 fusion.152
  164.7 1.2 convolution_add_fusion.2
  165.9 1.1 convolution_bitcast_fusion.9
  174.1 1.2 fusion.152
  175.3 1.2 convolution_add_fusion.2
  176.6 1.1 convolution_bitcast_fusion.9
  184.7 1.2 fusion.152
  185.9 1.2 convolution_add_fusion.2
  187.2 1.1 convolution_bitcast_fusion.9
  195.3 1.2 fusion.152
  196.5 1.2 convolution_add_fusion.2
  197.8 1.1 convolution_bitcast_fusion.9
  205.9 1.2 fusion.152
  207.2 1.2 convolution_add_fusion.2
  208.4 1.1 convolution_bitcast_fusion.9
  216.5 1.2 fusion.152
  217.8 1.2 convolution_add_fusion.2
  219.0 1.1 convolution_bitcast_fusion.9
  227.1 1.2 fusion.152
  228.4 1.2 convolution_add_fusion.2
  229.6 1.1 convolution_bitcast_fusion.9
  237.8 1.2 fusion.152
  239.0 1.2 convolution_add_fusion.2
  240.2 1.1 convolution_bitcast_fusion.9
  248.4 1.2 fusion.152
  249.6 1.2 convolution_add_fusion.2
  250.8 1.1 convolution_bitcast_fusion.9
  259.0 1.2 fusion.152
  260.2 1.2 convolution_add_fusion.2
  261.4 1.1 convolution_bitcast_fusion.9
  269.6 1.2 fusion.152
  270.8 1.2 convolution_add_fusion.2
  272.1 1.1 convolution_bitcast_fusion.9
  280.2 1.2 fusion.152
  281.4 1.2 convolution_add_fusion.2
  282.7 1.1 convolution_bitcast_fusion.9
  290.8 1.2 fusion.152
  292.0 1.2 convolution_add_fusion.2
  293.3 1.1 convolution_bitcast_fusion.9
  299.4 53.3 %all_to_all.63 = bf16[16,8,128,128]{3,1,0,2:T(8,128)(2,1)S(1)} all-to-all(bf16[16,8,128,128]{3,1,0,2:T(8,128)(2,1)} %get-tuple-element.69), channel_id=1, replica_groups=mesh['tm'=16,'space'=8] {'space'}, dimensions={2} | all-to-all | bytes 8388608 | tf_op jit(solution)/shard_map/all_to_all | solution.py:99
  352.7 4.9 %copy.38 = bf16[16,8,8,16,128]{4,3,2,1,0:T(8,128)(2,1)S(1)} copy(bf16[16,8,8,16,128]{4,2,0,3,1:T(8,128)(2,1)S(1)} %bitcast.142) | data formatting | bytes 8388608 | tf_op jit(solution)/shard_map/all_to_all | solution.py:99
  357.5 1.2 copy.39
  358.7 54.3 %all_to_all.64 = bf16[16,64,16,128]{3,2,0,1:T(8,128)(2,1)S(1)} all-to-all(bf16[16,64,16,128]{3,2,0,1:T(8,128)(2,1)S(1)} %copy.39), channel_id=1, replica_groups=mesh['tm'=16,'space'=8] {'tm'}, dimensions={1} | all-to-all | bytes 8388608 | tf_op jit(solution)/shard_map/all_to_all | solution.py:89
  415.3 1.7 copy.41
  417.4 21.2 %fusion.69 = bf16[256,4,16,128]{3,2,1,0:T(8,128)(2,1)} fusion(bf16[256,4,16,128]{3,2,1,0:T(8,128)(2,1)S(1)} %copy-done, f32[16,16,4,16,128]{4,3,2,1,0:T(8,128)S(1)} %copy.41, f32[256]{0:T(256)S(1)} %copy-done.2), kind=kLoop, calls=%fused_computation.81 | loop fusion | flops 142606336 | bytes 16778240 | tf_op jit(solution)/shard_map/convert_element_type | solution.py:118
  (227 shorter events, 114.7 us)
Async XLA Ops:
  0.0 7.1 %copy-start.1 = (bf16[16,64]{1,0:T(8,128)(2,1)S(1)}, bf16[16,64]{1,0:T(8,128)(2,1)}, u32[]{:S(2)}) copy-start(bf16[16,64]{1,0:T(8,128)(2,1)} %param.7) | copy-start | bytes 6148
  0.0 56.7 %all-to-all-start = ((bf16[256,4,16,128]{3,2,1,0:T(8,128)(2,1)}), bf16[256,4,16,128]{3,2,1,0:T(8,128)(2,1)}, u32[]{:S(2)}, u32[]{:S(2)}) async-start(bf16[256,4,16,128]{3,2,1,0:T(8,128)(2,1)} %param.6), calls=%async_computation | async-start | bytes 8388608 | tf_op jit(solution)/shard_map/all_to_all | solution.py:95
  67.1 57.1 %all-to-all-start.1 = ((bf16[16,64,16,128]{3,2,0,1:T(8,128)(2,1)}), bf16[16,64,16,128]{3,2,0,1:T(8,128)(2,1)}, u32[]{:S(2)}, u32[]{:S(2)}) async-start(bf16[16,64,16,128]{3,2,0,1:T(8,128)(2,1)} %copy.34), calls=%async_computation.1 | async-start | bytes 8388608 | tf_op jit(solution)/shard_map/all_to_all | solution.py:97
  415.2 2.2 copy-start
  415.3 2.2 copy-start.2
where the time goes:
time: 441 us; the launch traced here: 439 us
  matrix products  150 us (34%)
  blocking collectives  108 us (24%)
  waiting for transfers between devices  86.3 us (20%)
  local copies, waits for them, and re-layouts  51 us (12%)
  other arithmetic  27.4 us (6%)
  starting transfers between devices  14.3 us (3%)
    dot_general x96, matrix products, row_section(): return jnp.einsum('ah,mhk->mak', dft_table, operand, precision=three_pass)  76.9 us
    all_to_all x1, blocking collectives, final_layout(): lax.all_to_all(rows_back, 'tm', split_axis=1, concat_axis=0, tiled=True)  54.3 us
    all_to_all x1, blocking collectives, run_block(): lax.all_to_all(filtered, 'space', split_axis=2, concat_axis=1, tiled=True)  53.3 us
    all_to_all x1, waiting for transfers between devices, run_block(): lax.all_to_all(convolved, 'space', split_axis=1, concat_axis=2, tiled=True)  49.6 us
    all_to_all x1, waiting for transfers between devices, run_block(): lax.all_to_all(channel_block, 'tm', split_axis=0, concat_axis=1, tiled=True)  36.8 us
    convert_element_type x1, other arithmetic, local(): return jax.nn.gelu(pre_activation, approximate=False).astype(jnp.bfloat16)  21.2 us
    dot_general x16, matrix products, frame_spectrum(): jnp.einsum('mhw,wk->mhk', operand, forward_low, preferred_element_type=jn...  19.7 us
    dot_general x16, matrix products, frame_spectrum(): jnp.einsum('mhw,wk->mhk', operand, forward_high, preferred_element_type=j...  19.6 us
  transfers between devices with their start and end apart: 2, of which 2 were waited for; matrix products, arithmetic and copies ran while one was open for 3% of the time, Pallas kernels for 0%

commit v1 on v0

v1 whole, which is shorter than its diff:
```python
import functools
import math

import jax
import jax.numpy as jnp
import numpy as np
from jax import lax
from jax.experimental import pallas as pl
from jax.experimental.pallas import tpu as pltpu
from jax.sharding import PartitionSpec as P

AXES = ("tm", "space")
BLOCK = 16
GROUPS_PER_STEP = 4

ERF_TANH = (
    0.7978849411010742,
    0.03633308410644531,
    -3.259458389948122e-05,
    -5.530638009076938e-05,
    3.964782081311569e-06,
    -1.322666491887503e-07,
    1.7562715726171518e-09,
)


def dft_tables(length):
    positions = np.arange(length)
    angles = (positions[:, None] * positions[None, :] % length) * (2.0 * math.pi / length)
    cos, sin = np.cos(angles), np.sin(angles)
    forward = np.block([[cos, -sin], [sin, cos]])
    return forward.astype(np.float32), forward.T.copy().astype(np.float32)


def prepare_kernel(picked_ref, kernel_ref, forward_ref, backward_ref, time_ref, spec_ref):
    rows, cols = time_ref.shape[1], time_ref.shape[2]
    frames = picked_ref.shape[2]

    def spread(shape, along):
        wide = lax.broadcasted_iota(jnp.int32, shape, along) // BLOCK
        return (wide == lax.broadcasted_iota(jnp.int32, shape, 1 - along)).astype(jnp.bfloat16)

    tall = jnp.dot(
        spread((rows, BLOCK), 0), picked_ref[0], preferred_element_type=jnp.float32
    ).astype(jnp.bfloat16)
    full = jnp.dot(tall, spread((frames, cols), 1), preferred_element_type=jnp.float32)
    row_of = lax.broadcasted_iota(jnp.int32, (rows, cols), 0) % BLOCK
    col_of = lax.broadcasted_iota(jnp.int32, (rows, cols), 1) % BLOCK
    time_ref[0] = jnp.where(row_of == col_of, full, 0.0).astype(jnp.bfloat16)

    size = kernel_ref.shape[1]
    exact = lax.Precision.HIGHEST
    half = jnp.dot(
        kernel_ref[0], forward_ref[:size, :], precision=exact, preferred_element_type=jnp.float32
    )
    stacked = jnp.concatenate([half[:, :size], half[:, size:]], axis=0)
    spec = jnp.dot(
        backward_ref[...], stacked, precision=exact, preferred_element_type=jnp.float32
    )
    spec_ref[0] = spec * (1.0 / (size * size))


def gelu(pre):
    square = pre * pre
    q = jnp.float32(ERF_TANH[-1])
    for coefficient in ERF_TANH[-2::-1]:
        q = q * square + jnp.float32(coefficient)
    return 0.5 * pre * (1.0 + jnp.tanh(pre * q))


def filter_kernel(x_ref, time_ref, spec_ref, gain_ref, forward_ref, backward_ref, o_ref, conv):
    tm, space = x_ref.shape[0], x_ref.shape[1]
    per_device = x_ref.shape[3]
    frames, size, _ = conv.shape
    block_rows = BLOCK * BLOCK
    blocks = frames // BLOCK
    devices = BLOCK // per_device

    for pair in range(space // 2):
        for block in range(blocks):
            sources = devices * (block + 1)
            sides = [
                x_ref[0:sources, 2 * pair + side, 0].reshape(block_rows * (block + 1), size)
                for side in range(2)
            ]
            summed = jnp.dot(
                time_ref[0, :, (blocks - 1 - block) * block_rows :],
                jnp.concatenate(sides, axis=1),
                preferred_element_type=jnp.float32,
            ).astype(jnp.bfloat16)
            for side in range(2):
                first = (2 * pair + side) * BLOCK
                conv[block * BLOCK : (block + 1) * BLOCK, first : first + BLOCK, :] = summed[
                    :, side * size : (side + 1) * size
                ].reshape(BLOCK, BLOCK, size)

    gain = gain_ref[0, 0, 0]
    forward = forward_ref[...]
    backward = backward_ref[...]
    group_count = GROUPS_PER_STEP
    pair_count = 2 * group_count

    def stack_rows(value):
        parts = [value[p * size : (p + 1) * size] for p in range(pair_count)]
        return jnp.concatenate(
            [
                jnp.concatenate([part[:, :size] for part in parts], axis=1),
                jnp.concatenate([part[:, size:] for part in parts], axis=1),
            ],
            axis=0,
        )

    def stack_cols(value):
        return jnp.concatenate(
            [
                jnp.concatenate(
                    [
                        value[:size, p * size : (p + 1) * size],
                        value[size:, p * size : (p + 1) * size],
                    ],
                    axis=1,
                )
                for p in range(pair_count)
            ],
            axis=0,
        )

    def dot(a, b):
        return jnp.dot(a, b, preferred_element_type=jnp.float32)

    def step(index, carry):
        start = index * (4 * group_count)
        pairs = [
            jnp.concatenate([conv[start + 2 * p], conv[start + 2 * p + 1]], axis=1)
            for p in range(pair_count)
        ]
        cols = dot(jnp.concatenate(pairs, axis=0), forward).astype(jnp.bfloat16)
        spectrum = dot(backward, stack_rows(cols))
        spec_re = jnp.concatenate([spec_ref[0, :size]] * pair_count, axis=1)
        spec_im = jnp.concatenate([spec_ref[0, size:]] * pair_count, axis=1)
        re, im = spectrum[:size], spectrum[size:]
        product = jnp.concatenate(
            [re * spec_re - im * spec_im, re * spec_im + im * spec_re], axis=0
        ).astype(jnp.bfloat16)
        restored = dot(forward, product).astype(jnp.bfloat16)
        result = dot(stack_cols(restored), backward).astype(jnp.bfloat16)
        for group in range(group_count):
            device = index * group_count + group
            for frame in range(per_device):
                p, side = (4 * group + frame) // 2, frame % 2
                filtered = result[p * size : (p + 1) * size, side * size : (side + 1) * size]
                latent = x_ref[device, :, 0, frame].reshape(size, size)
                pre = filtered.astype(jnp.float32) + gain * latent.astype(jnp.float32)
                o_ref[device, :, 0, frame] = gelu(pre).astype(jnp.bfloat16).reshape(
                    space, BLOCK, size
                )
        return carry

    lax.fori_loop(0, tm // group_count, step, 0)


def local(latents, time_taps, space_taps, skip_gain):
    tm, space = lax.axis_size("tm"), lax.axis_size("space")
    channels, per_device, rows, size = latents.shape
    frames = tm * per_device
    own = channels // (tm * space)
    here = lax.axis_index("space") * own

    received = lax.all_to_all(latents, AXES, split_axis=0, concat_axis=0, tiled=True)
    received = received.reshape(tm, space, own, per_device, rows, size)

    taps = lax.dynamic_slice_in_dim(time_taps, here, own, 0)
    kernels = lax.dynamic_slice_in_dim(space_taps, here, own, 0)
    gains = lax.dynamic_slice_in_dim(skip_gain, lax.axis_index("tm") * own * space + here, own, 0)
    lag = (
        (frames - BLOCK)
        + lax.broadcasted_iota(jnp.int32, (frames, BLOCK, frames), 1)
        - lax.broadcasted_iota(jnp.int32, (frames, BLOCK, frames), 2)
    )
    chosen = lag == lax.broadcasted_iota(jnp.int32, (frames, BLOCK, frames), 0)
    picked = jnp.sum(
        jnp.where(chosen[None], taps.astype(jnp.float32)[:, :, None, None], 0.0), axis=1
    ).astype(jnp.bfloat16)

    forward, backward = (jnp.asarray(table) for table in dft_tables(size))
    wide = BLOCK * BLOCK
    time_matrix, spectra = pl.pallas_call(
        prepare_kernel,
        grid=(own,),
        in_specs=[
            pl.BlockSpec((1, BLOCK, frames), lambda k: (k, 0, 0)),
            pl.BlockSpec((1, size, size), lambda k: (k, 0, 0)),
            pl.BlockSpec((2 * size, 2 * size), lambda k: (0, 0)),
            pl.BlockSpec((2 * size, 2 * size), lambda k: (0, 0)),
        ],
        out_specs=[
            pl.BlockSpec((1, wide, frames * BLOCK), lambda k: (k, 0, 0)),
            pl.BlockSpec((1, 2 * size, size), lambda k: (k, 0, 0)),
        ],
        out_shape=[
            jax.ShapeDtypeStruct((own, wide, frames * BLOCK), jnp.bfloat16),
            jax.ShapeDtypeStruct((own, 2 * size, size), jnp.float32),
        ],
        name="prepare",
    )(picked, kernels, forward, backward)

    block = (tm, space, 1, per_device, rows, size)
    filtered = pl.pallas_call(
        filter_kernel,
        grid=(own,),
        in_specs=[
            pl.BlockSpec(block, lambda k: (0, 0, k, 0, 0, 0)),
            pl.BlockSpec((1, wide, frames * BLOCK), lambda k: (k, 0, 0)),
            pl.BlockSpec((1, 2 * size, size), lambda k: (k, 0, 0)),
            pl.BlockSpec((1, 1, 1), lambda k: (k, 0, 0), memory_space=pltpu.SMEM),
            pl.BlockSpec((2 * size, 2 * size), lambda k: (0, 0)),
            pl.BlockSpec((2 * size, 2 * size), lambda k: (0, 0)),
        ],
        out_specs=pl.BlockSpec(block, lambda k: (0, 0, k, 0, 0, 0)),
        out_shape=jax.ShapeDtypeStruct(received.shape, jnp.bfloat16),
        scratch_shapes=[pltpu.VMEM((frames, size, size), jnp.bfloat16)],
        compiler_params=pltpu.CompilerParams(vmem_limit_bytes=48 * 1024 * 1024),
        name="filter",
    )(
        received,
        time_matrix,
        spectra,
        gains.reshape(own, 1, 1),
        forward.astype(jnp.bfloat16),
        backward.astype(jnp.bfloat16),
    )
    return lax.all_to_all(
        filtered.reshape(latents.shape), AXES, split_axis=0, concat_axis=0, tiled=True
    )


def solution(mesh):
    in_specs = (P(None, "tm", "space", None), P("tm", None), P("tm", None, None), P())
    out_specs = P(None, "tm", "space", None)
    return jax.shard_map(local, mesh=mesh, in_specs=in_specs, out_specs=out_specs, check_vma=False)
```

time: 441 us -> 143 us (0.32)
  matrix products: 150 us -> 0 us
  blocking collectives: 108 us -> 57.1 us
  local copies, waits for them, and re-layouts: 51 us -> 5.05 us
  waiting for transfers between devices: 86.3 us -> 45.1 us
  other arithmetic: 27.4 us -> 1.62 us
  Pallas kernels: 0 us -> 21.7 us
    dot_general x161 -> x0, matrix products: 150 us -> none  [the longest x96 76.9 us: row_section(): return jnp.einsum('ah,mhk->mak', dft_table, operand, precision=three_pass)]
    all_to_all x2 -> x1, blocking collectives: 108 us -> 57.1 us  [local(): lax.all_to_all(filtered.reshape(latents.shape), AXES, split_axis=0, conca...]
    all_to_all x2 -> x1, waiting for transfers between devices: 86.3 us -> 45.1 us  [local(): lax.all_to_all(latents, AXES, split_axis=0, concat_axis=0, tiled=True)]
    pallas_call x0 -> x2, Pallas kernels: none -> 21.7 us  [the longest x1 17.6 us: local(): pl.pallas_call(filter_kernel, grid=(own,), in_specs=[pl.BlockSpec(block,...]
    convert_element_type x4 -> x1, other arithmetic: 22.3 us -> 0.69 us  [local(): taps.astype(jnp.float32)[:, :, None, None]]
    all_to_all x5 -> x0, local copies, waits for them, and re-layouts: 17 us -> none  [the longest x2 6.07 us: run_block(): lax.all_to_all(filtered, 'space', split_axis=2, concat_axis=1, tiled=True)]
    dynamic_update_slice x16 -> x0, local copies, waits for them, and re-layouts: 14.1 us -> none  [spatial_filter(): return lax.map(one_channel, (frames, kernels))]
    gather x2 -> x0, local copies, waits for them, and re-layouts: 12.7 us -> none  [causal_matrix(): picked = jnp.take(taps, jnp.maximum(offset, 0), axis=1)]
  transfers between devices with their start and end apart: 2 -> 1, of which waited for: 2 -> 1; matrix products, arithmetic and copies ran while one was open for 3% -> 2% of each run, Pallas kernels for 0% -> 3%
where the time goes in v1:
time: 143 us
  blocking collectives  57.1 us (40%)
  waiting for transfers between devices  45.1 us (32%)
  Pallas kernels  21.7 us (15%)
  starting transfers between devices  12 us (8%)
  local copies, waits for them, and re-layouts  5.05 us (4%)
  other arithmetic  1.62 us (1%)
    all_to_all x1, blocking collectives, local(): lax.all_to_all(filtered.reshape(latents.shape), AXES, split_axis=0, conca...  57.1 us
    all_to_all x1, waiting for transfers between devices, local(): lax.all_to_all(latents, AXES, split_axis=0, concat_axis=0, tiled=True)  45.1 us
    pallas_call x1, Pallas kernels, local(): pl.pallas_call(filter_kernel, grid=(own,), in_specs=[pl.BlockSpec(block,...  17.6 us
    all_to_all x1, starting transfers between devices, local(): lax.all_to_all(latents, AXES, split_axis=0, concat_axis=0, tiled=True)  12 us
    unnamed x13, local copies, waits for them, and re-layouts  4.2 us
    pallas_call x1, Pallas kernels, local(): pl.pallas_call(prepare_kernel, grid=(own,), in_specs=[pl.BlockSpec((1, BL...  4.12 us
  transfers between devices with their start and end apart: 1, of which 1 were waited for; matrix products, arithmetic and copies ran while one was open for 2% of the time, Pallas kernels for 3%

profile of v1, /device:TPU:1, one launch (start us, length us, event | category | flops | bytes accessed | tf_op | source)
XLA Modules:
  0.0 142.7 jit_solution(16364922871432312124)
XLA Ops:
  0.0 0.0 copy-start
  0.0 0.0 copy-start.3
  0.0 0.0 copy-start.4
  0.0 0.0 copy-start.5
  0.0 12.0 %all-to-all-start = ((bf16[256,4,16,128]{3,2,1,0:T(8,128)(2,1)}), bf16[256,4,16,128]{3,2,1,0:T(8,128)(2,1)}, u32[]{:S(2)}, u32[]{:S(2)}) async-start(bf16[256,4,16,128]{3,2,1,0:T(8,128)(2,1)} %param.6), calls=%async_computation | async-start | bytes 8388608 | tf_op jit(solution)/shard_map/all_to_all | solution.py:169
  12.0 0.0 copy-done.5
  12.0 0.1 dynamic-slice_bitcast_fusion
  12.1 0.1 copy.8.gain_ref
  12.2 0.7 dynamic-slice_convert_fusion
  12.9 0.0 copy-done
  12.9 0.7 constant_dynamic-slice_fusion.kernel_ref
  13.6 0.1 iota_compare_fusion
  13.7 0.8 select_reduce_fusion.picked_ref
  14.5 4.1 %prepare.1 = (bf16[2,256,1024]{2,1,0:T(8,128)(2,1)}, f32[2,256,128]{2,1,0:T(8,128)}) custom-call(bf16[2,16,64]{2,1,0:T(8,128)(2,1)} %select_reduce_fusion.picked_ref, f32[2,128,128]{2,1,0:T(8,128)} %constant_dynamic-slice_fusion.kernel_ref, f32[256,256]{1,0:T(8,128)} %constant.27.clone.forward_ref, f32[256,256]{1,0:T(8,128)} %constant.28.clone.backward_ref), custom_call_target="tpu_custom_call" | custom-call | tf_op jit(solution)/shard_map/prepare/pallas_call | solution.py:187
  18.6 45.1 %all-to-all-done = bf16[256,4,16,128]{3,2,1,0:T(8,128)(2,1)} async-done(((bf16[256,4,16,128]{3,2,1,0:T(8,128)(2,1)}), bf16[256,4,16,128]{3,2,1,0:T(8,128)(2,1)}, u32[]{:S(2)}, u32[]{:S(2)}) %all-to-all-start) | async-done | bytes 4194336 | tf_op jit(solution)/shard_map/all_to_all | solution.py:169
  63.8 0.0 copy-done.3
  63.8 0.0 copy-done.4
  63.8 0.0 copy-start.1
  63.8 1.2 copy-done.1
  65.0 0.0 copy-start.2
  65.0 0.9 copy-done.2
  65.9 17.6 %filter.1 = bf16[16,8,2,4,16,128]{5,4,3,2,1,0:T(8,128)(2,1)S(1)} custom-call(bf16[16,8,2,4,16,128]{5,4,3,2,1,0:T(8,128)(2,1)} %bitcast.x_ref, bf16[2,256,1024]{2,1,0:T(8,128)(2,1)S(1)} %copy-done.1, f32[2,256,128]{2,1,0:T(8,128)S(1)} %copy-done.2, f32[2,1,1]{2,1,0:T(1,128)S(1)} %copy.8.gain_ref, bf16[256,256]{1,0:T(8,128)(2,1)S(1)} %copy-done.4, ...), custom_call_target="tpu_custom_call" | custom-call | tf_op jit(solution)/shard_map/filter/pallas_call | solution.py:208
  83.6 57.1 %all_to_all.10 = bf16[256,4,16,128]{3,2,1,0:T(8,128)(2,1)S(1)} all-to-all(bf16[256,4,16,128]{3,2,1,0:T(8,128)(2,1)S(1)} %bitcast.4), channel_id=1, replica_groups=mesh['tm'=16,'space'=8] {'tm','space'}, dimensions={0} | all-to-all | bytes 8388608 | tf_op jit(solution)/shard_map/all_to_all | solution.py:232
  140.7 2.0 %copy.10 = bf16[256,4,16,128]{3,2,1,0:T(8,128)(2,1)} copy(bf16[256,4,16,128]{3,2,1,0:T(8,128)(2,1)S(1)} %all_to_all.10) | data formatting | bytes 8388608
  (1 shorter events, 0.0 us)
Async XLA Ops:
  0.0 12.9 %copy-start = (f32[16,128,128]{2,1,0:T(8,128)S(1)}, f32[16,128,128]{2,1,0:T(8,128)}, u32[]{:S(2)}) copy-start(f32[16,128,128]{2,1,0:T(8,128)} %param.8) | copy-start | bytes 3145732
  0.0 63.8 %copy-start.3 = (bf16[256,256]{1,0:T(8,128)(2,1)S(1)}, bf16[256,256]{1,0:T(8,128)(2,1)}, u32[]{:S(2)}) copy-start(bf16[256,256]{1,0:T(8,128)(2,1)} %constant.31.backward_ref) | copy-start | bytes 393220
  0.0 63.8 %copy-start.4 = (bf16[256,256]{1,0:T(8,128)(2,1)S(1)}, bf16[256,256]{1,0:T(8,128)(2,1)}, u32[]{:S(2)}) copy-start(bf16[256,256]{1,0:T(8,128)(2,1)} %constant.30.forward_ref) | copy-start | bytes 393220
  0.0 12.0 %copy-start.5 = (f32[256]{0:T(256)S(1)}, f32[256]{0:T(256)}, u32[]{:S(2)}) copy-start(f32[256]{0:T(256)} %param.9) | copy-start | bytes 3076
  0.0 63.7 %all-to-all-start = ((bf16[256,4,16,128]{3,2,1,0:T(8,128)(2,1)}), bf16[256,4,16,128]{3,2,1,0:T(8,128)(2,1)}, u32[]{:S(2)}, u32[]{:S(2)}) async-start(bf16[256,4,16,128]{3,2,1,0:T(8,128)(2,1)} %param.6), calls=%async_computation | async-start | bytes 8388608 | tf_op jit(solution)/shard_map/all_to_all | solution.py:169
  63.8 1.2 copy-start.1
  65.0 0.9 copy-start.2

commit v2 on v1

--- a/solution.py
+++ b/solution.py
@@ -1,4 +1,3 @@
-import functools
 import math
 
 import jax
@@ -11,17 +10,7 @@
 
 AXES = ("tm", "space")
 BLOCK = 16
-GROUPS_PER_STEP = 4
-
-ERF_TANH = (
-    0.7978849411010742,
-    0.03633308410644531,
-    -3.259458389948122e-05,
-    -5.530638009076938e-05,
-    3.964782081311569e-06,
-    -1.322666491887503e-07,
-    1.7562715726171518e-09,
-)
+GROUPS_PER_STEP = 16
 
 
 def dft_tables(length):
@@ -61,11 +50,7 @@
 
 
 def gelu(pre):
-    square = pre * pre
-    q = jnp.float32(ERF_TANH[-1])
-    for coefficient in ERF_TANH[-2::-1]:
-        q = q * square + jnp.float32(coefficient)
-    return 0.5 * pre * (1.0 + jnp.tanh(pre * q))
+    return 0.5 * pre * (1.0 + lax.erf(pre * math.sqrt(0.5)))
 
 
 def filter_kernel(x_ref, time_ref, spec_ref, gain_ref, forward_ref, backward_ref, o_ref, conv):
@@ -143,14 +128,14 @@
             [re * spec_re - im * spec_im, re * spec_im + im * spec_re], axis=0
         ).astype(jnp.bfloat16)
         restored = dot(forward, product).astype(jnp.bfloat16)
-        result = dot(stack_cols(restored), backward).astype(jnp.bfloat16)
+        result = dot(stack_cols(restored), backward)
         for group in range(group_count):
             device = index * group_count + group
             for frame in range(per_device):
                 p, side = (4 * group + frame) // 2, frame % 2
                 filtered = result[p * size : (p + 1) * size, side * size : (side + 1) * size]
                 latent = x_ref[device, :, 0, frame].reshape(size, size)
-                pre = filtered.astype(jnp.float32) + gain * latent.astype(jnp.float32)
+                pre = filtered + gain * latent.astype(jnp.float32)
                 o_ref[device, :, 0, frame] = gelu(pre).astype(jnp.bfloat16).reshape(
                     space, BLOCK, size
                 )
@@ -219,7 +204,7 @@
         out_specs=pl.BlockSpec(block, lambda k: (0, 0, k, 0, 0, 0)),
         out_shape=jax.ShapeDtypeStruct(received.shape, jnp.bfloat16),
         scratch_shapes=[pltpu.VMEM((frames, size, size), jnp.bfloat16)],
-        compiler_params=pltpu.CompilerParams(vmem_limit_bytes=48 * 1024 * 1024),
+        compiler_params=pltpu.CompilerParams(vmem_limit_bytes=60 * 1024 * 1024),
         name="filter",
     )(
         received,

time: 143 us -> 136 us (0.951)
  Pallas kernels: 21.7 us -> 16.5 us
  local copies, waits for them, and re-layouts: 5.05 us -> 3.44 us
    pallas_call x1, Pallas kernels: 17.6 us -> 12.4 us  [local(): pl.pallas_call(filter_kernel, grid=(own,), in_specs=[pl.BlockSpec(block,...]
    unnamed x13 -> x5, local copies, waits for them, and re-layouts: 4.2 us -> 2.02 us
where the time goes in v2:
time: 136 us
  blocking collectives  57.3 us (42%)
  waiting for transfers between devices  44.6 us (33%)
  Pallas kernels  16.5 us (12%)
  starting transfers between devices  12 us (9%)
  local copies, waits for them, and re-layouts  3.44 us (3%)
  other arithmetic  1.63 us (1%)
    all_to_all x1, blocking collectives, local(): lax.all_to_all(filtered.reshape(latents.shape), AXES, split_axis=0, conca...  57.3 us
    all_to_all x1, waiting for transfers between devices, local(): lax.all_to_all(latents, AXES, split_axis=0, concat_axis=0, tiled=True)  44.6 us
    pallas_call x1, Pallas kernels, local(): pl.pallas_call(filter_kernel, grid=(own,), in_specs=[pl.BlockSpec(block,...  12.4 us
    all_to_all x1, starting transfers between devices, local(): lax.all_to_all(latents, AXES, split_axis=0, concat_axis=0, tiled=True)  12 us
    pallas_call x1, Pallas kernels, local(): pl.pallas_call(prepare_kernel, grid=(own,), in_specs=[pl.BlockSpec((1, BL...  4.1 us
  transfers between devices with their start and end apart: 1, of which 1 were waited for; matrix products, arithmetic and copies ran while one was open for 2% of the time, Pallas kernels for 3%

profile of v2, /device:TPU:1, one launch (start us, length us, event | category | flops | bytes accessed | tf_op | source)
XLA Modules:
  0.0 135.5 jit_solution(7967533842307751948)
XLA Ops:
  0.0 0.0 copy-start
  0.0 0.0 copy-start.1
  0.0 12.0 %all-to-all-start = ((bf16[256,4,16,128]{3,2,1,0:T(8,128)(2,1)}), bf16[256,4,16,128]{3,2,1,0:T(8,128)(2,1)}, u32[]{:S(2)}, u32[]{:S(2)}) async-start(bf16[256,4,16,128]{3,2,1,0:T(8,128)(2,1)} %param.6), calls=%async_computation | async-start | bytes 8388608 | tf_op jit(solution)/shard_map/all_to_all | solution.py:154
  12.0 0.0 copy-done.1
  12.0 0.1 dynamic-slice_bitcast_fusion
  12.1 0.7 copy.8.gain_ref
  12.7 0.7 dynamic-slice_convert_fusion
  13.4 0.0 copy-done
  13.4 0.7 constant_dynamic-slice_fusion.kernel_ref
  14.1 0.1 iota_compare_fusion
  14.2 0.8 select_reduce_fusion.picked_ref
  15.0 4.1 %prepare.1 = (bf16[2,256,1024]{2,1,0:T(8,128)(2,1)}, f32[2,256,128]{2,1,0:T(8,128)}) custom-call(bf16[2,16,64]{2,1,0:T(8,128)(2,1)} %select_reduce_fusion.picked_ref, f32[2,128,128]{2,1,0:T(8,128)} %constant_dynamic-slice_fusion.kernel_ref, f32[256,256]{1,0:T(8,128)} %constant.27.clone.forward_ref, f32[256,256]{1,0:T(8,128)} %constant.28.clone.backward_ref), custom_call_target="tpu_custom_call" | custom-call | tf_op jit(solution)/shard_map/prepare/pallas_call | solution.py:172
  19.1 44.6 %all-to-all-done = bf16[256,4,16,128]{3,2,1,0:T(8,128)(2,1)} async-done(((bf16[256,4,16,128]{3,2,1,0:T(8,128)(2,1)}), bf16[256,4,16,128]{3,2,1,0:T(8,128)(2,1)}, u32[]{:S(2)}, u32[]{:S(2)}) %all-to-all-start) | async-done | bytes 4194336 | tf_op jit(solution)/shard_map/all_to_all | solution.py:154
  63.7 12.4 %filter.1 = bf16[16,8,2,4,16,128]{5,4,3,2,1,0:T(8,128)(2,1)} custom-call(bf16[16,8,2,4,16,128]{5,4,3,2,1,0:T(8,128)(2,1)} %bitcast.x_ref, bf16[2,256,1024]{2,1,0:T(8,128)(2,1)} %get-tuple-element.7.time_ref, f32[2,256,128]{2,1,0:T(8,128)} %get-tuple-element.8.spec_ref, f32[2,1,1]{2,1,0:T(1,128)} %copy.8.gain_ref, bf16[256,256]{1,0:T(8,128)(2,1)} %constant.30.forward_ref, ...), custom_call_target="tpu_custom_call" | custom-call | tf_op jit(solution)/shard_map/filter/pallas_call | solution.py:193
  76.2 57.3 %all_to_all.10 = bf16[256,4,16,128]{3,2,1,0:T(8,128)(2,1)S(1)} all-to-all(bf16[256,4,16,128]{3,2,1,0:T(8,128)(2,1)} %bitcast.4), channel_id=1, replica_groups=mesh['tm'=16,'space'=8] {'tm','space'}, dimensions={0} | all-to-all | bytes 8388608 | tf_op jit(solution)/shard_map/all_to_all | solution.py:217
  133.5 2.0 %copy.10 = bf16[256,4,16,128]{3,2,1,0:T(8,128)(2,1)} copy(bf16[256,4,16,128]{3,2,1,0:T(8,128)(2,1)S(1)} %all_to_all.10) | data formatting | bytes 8388608
  (1 shorter events, 0.0 us)
Async XLA Ops:
  0.0 13.4 %copy-start = (f32[16,128,128]{2,1,0:T(8,128)S(1)}, f32[16,128,128]{2,1,0:T(8,128)}, u32[]{:S(2)}) copy-start(f32[16,128,128]{2,1,0:T(8,128)} %param.8) | copy-start | bytes 3145732
  0.0 12.0 %copy-start.1 = (f32[256]{0:T(256)S(1)}, f32[256]{0:T(256)}, u32[]{:S(2)}) copy-start(f32[256]{0:T(256)} %param.9) | copy-start | bytes 3076
  0.0 63.7 %all-to-all-start = ((bf16[256,4,16,128]{3,2,1,0:T(8,128)(2,1)}), bf16[256,4,16,128]{3,2,1,0:T(8,128)(2,1)}, u32[]{:S(2)}, u32[]{:S(2)}) async-start(bf16[256,4,16,128]{3,2,1,0:T(8,128)(2,1)} %param.6), calls=%async_computation | async-start | bytes 8388608 | tf_op jit(solution)/shard_map/all_to_all | solution.py:154

commit v3 on v2

v3 whole, which is shorter than its diff:
```python
import math

import jax
import jax.numpy as jnp
import numpy as np
from jax import lax
from jax.experimental import pallas as pl
from jax.experimental.pallas import tpu as pltpu
from jax.sharding import PartitionSpec as P

AXES = ("tm", "space")
TILE = 8
BLOCK = 32
PARTS = 4
VMEM_LIMIT = 56 * 1024 * 1024


def dft_tables(length):
    positions = np.arange(length)
    angles = (positions[:, None] * positions[None, :] % length) * (2.0 * math.pi / length)
    cos, sin = np.cos(angles), np.sin(angles)
    forward = np.block([[cos, -sin], [sin, cos]])
    return forward.astype(np.float32), forward.T.copy().astype(np.float32)


def prepare_kernel(picked_ref, kernel_ref, forward_ref, backward_ref, time_ref, spec_ref):
    rows, cols = time_ref.shape[1], time_ref.shape[2]
    frames = picked_ref.shape[2]

    def spread(shape, along):
        wide = lax.broadcasted_iota(jnp.int32, shape, along) // TILE
        return (wide == lax.broadcasted_iota(jnp.int32, shape, 1 - along)).astype(jnp.bfloat16)

    tall = jnp.dot(
        spread((rows, BLOCK), 0), picked_ref[0], preferred_element_type=jnp.float32
    ).astype(jnp.bfloat16)
    full = jnp.dot(tall, spread((frames, cols), 1), preferred_element_type=jnp.float32)
    row_of = lax.broadcasted_iota(jnp.int32, (rows, cols), 0) % TILE
    col_of = lax.broadcasted_iota(jnp.int32, (rows, cols), 1) % TILE
    time_ref[0] = jnp.where(row_of == col_of, full, 0.0).astype(jnp.bfloat16)

    size = kernel_ref.shape[1]
    exact = lax.Precision.HIGHEST
    half = jnp.dot(
        kernel_ref[0], forward_ref[:size, :], precision=exact, preferred_element_type=jnp.float32
    )
    stacked = jnp.concatenate([half[:, :size], half[:, size:]], axis=0)
    spec = jnp.dot(
        backward_ref[...], stacked, precision=exact, preferred_element_type=jnp.float32
    )
    spec_ref[0] = spec * (math.sqrt(0.5) / (size * size))


def gelu_of_scaled(scaled):
    half = scaled * math.sqrt(0.5)
    return half + half * lax.erf(scaled)


def filter_kernel(
    x_hbm, time_hbm, spec_hbm, gain_ref, tables_hbm, o_ref,
    x_ref, time_ref, spec_ref, tables_ref, conv, result_a, result_b, in_sems,
):
    own, tm, space, per_device, rows, size = x_ref.shape
    frames = tm * per_device
    side_rows = BLOCK * TILE
    blocks = frames // BLOCK
    pieces = space // 2
    pairs = frames // 2
    devices = tm // (2 * PARTS)
    results = (result_a, result_b)

    def arrival(k, piece):
        return pltpu.make_async_copy(
            x_hbm.at[:, pl.ds(2 * piece, 2), k],
            x_ref.at[k, :, pl.ds(2 * piece, 2)],
            in_sems.at[k * pieces + piece],
        )

    def time_arrival(k):
        return pltpu.make_async_copy(
            time_hbm.at[k], time_ref.at[k], in_sems.at[own * pieces + k]
        )

    others = [
        pltpu.make_async_copy(tables_hbm, tables_ref, in_sems.at[own * pieces + own]),
        pltpu.make_async_copy(spec_hbm, spec_ref, in_sems.at[own * pieces + own + 1]),
    ]

    for k in range(own):
        time_arrival(k).start()
        for piece in range(pieces):
            arrival(k, piece).start()
        if k == 0:
            for other in others:
                other.start()

    def dot(a, b):
        return jnp.dot(a, b, preferred_element_type=jnp.float32)

    def over_time(k, piece):
        sides = [
            x_ref[k, :, 2 * piece + side].reshape(frames, rows, size) for side in range(2)
        ]
        halves = [
            jnp.concatenate(
                [
                    side[:, first : first + TILE].reshape(frames * TILE, size)
                    for side in sides
                ],
                axis=1,
            )
            for first in range(0, rows, TILE)
        ]
        for block in range(blocks):
            summed = jnp.concatenate(
                [
                    dot(
                        time_ref[k, :, (blocks - 1 - block) * side_rows :],
                        half[: (block + 1) * side_rows],
                    ).reshape(BLOCK, TILE, 2 * size)
                    for half in halves
                ],
                axis=1,
            ).astype(jnp.bfloat16)
            for side in range(2):
                conv[block * BLOCK : (block + 1) * BLOCK, 2 * piece + side] = summed[
                    :, :, side * size : (side + 1) * size
                ]

    def stack_rows(value):
        parts = [value[p * size : (p + 1) * size] for p in range(pairs)]
        return jnp.concatenate(
            [
                jnp.concatenate([part[:, :size] for part in parts], axis=1),
                jnp.concatenate([part[:, size:] for part in parts], axis=1),
            ],
            axis=0,
        )

    def stack_cols(value):
        return jnp.concatenate(
            [
                jnp.concatenate(
                    [
                        value[:size, p * size : (p + 1) * size],
                        value[size:, p * size : (p + 1) * size],
                    ],
                    axis=1,
                )
                for p in range(pairs)
            ],
            axis=0,
        )

    def over_space(k):
        forward, backward = tables_ref[0], tables_ref[1]
        images = jnp.concatenate(
            [
                jnp.concatenate(
                    [conv[2 * p + side].reshape(size, size) for side in range(2)], axis=1
                )
                for p in range(pairs)
            ],
            axis=0,
        )
        cols = dot(images, forward).astype(jnp.bfloat16)
        spectrum = dot(backward, stack_rows(cols))
        spec_re = jnp.concatenate([spec_ref[k, :size]] * pairs, axis=1)
        spec_im = jnp.concatenate([spec_ref[k, size:]] * pairs, axis=1)
        re, im = spectrum[:size], spectrum[size:]
        product = jnp.concatenate(
            [re * spec_re - im * spec_im, re * spec_im + im * spec_re], axis=0
        ).astype(jnp.bfloat16)
        restored = stack_cols(dot(forward, product).astype(jnp.bfloat16))
        for half in range(2):
            side = pairs // 2 * size
            results[half][...] = dot(restored[half * side : (half + 1) * side], backward)

    def finish(k, half, part):
        gain = gain_ref[k, 0, 0] * math.sqrt(0.5)
        for place in range(part * devices * per_device, (part + 1) * devices * per_device):
            device, frame = place // per_device, place % per_device
            p, side = place // 2, place % 2
            filtered = results[half][p * size : (p + 1) * size, side * size : (side + 1) * size]
            source = half * (tm // 2) + device
            latent = x_ref[k, source, :, frame].reshape(size, size).astype(jnp.float32)
            o_ref[source, :, k, frame] = (
                gelu_of_scaled(filtered + gain * latent)
                .astype(jnp.bfloat16)
                .reshape(space, rows, size)
            )

    def time_all(k):
        time_arrival(k).wait()
        for piece in range(pieces):
            arrival(k, piece).wait()
        for piece in range(pieces):
            over_time(k, piece)

    def finish_half(k, half):
        for part in range(PARTS):
            finish(k, half, part)

    time_all(0)
    for other in others:
        other.wait()
    for k in range(own):
        over_space(k)
        finish_half(k, 0)
        if k + 1 < own:
            time_all(k + 1)
        finish_half(k, 1)


def local(latents, time_taps, space_taps, skip_gain):
    tm, space = lax.axis_size("tm"), lax.axis_size("space")
    channels, per_device, rows, size = latents.shape
    frames = tm * per_device
    own = channels // (tm * space)
    here = lax.axis_index("space") * own

    received = lax.all_to_all(latents, AXES, split_axis=0, concat_axis=0, tiled=True)
    received = received.reshape(tm, space, own, per_device, rows, size)

    taps = lax.dynamic_slice_in_dim(time_taps, here, own, 0)
    kernels = lax.dynamic_slice_in_dim(space_taps, here, own, 0)
    gains = lax.dynamic_slice_in_dim(skip_gain, lax.axis_index("tm") * own * space + here, own, 0)
    lag = (
        (frames - BLOCK)
        + lax.broadcasted_iota(jnp.int32, (frames, BLOCK, frames), 1)
        - lax.broadcasted_iota(jnp.int32, (frames, BLOCK, frames), 2)
    )
    chosen = lag == lax.broadcasted_iota(jnp.int32, (frames, BLOCK, frames), 0)
    picked = jnp.sum(
        jnp.where(chosen[None], taps.astype(jnp.float32)[:, :, None, None], 0.0), axis=1
    ).astype(jnp.bfloat16)

    forward, backward = (jnp.asarray(table) for table in dft_tables(size))
    wide = BLOCK * TILE
    time_matrix, spectra = pl.pallas_call(
        prepare_kernel,
        grid=(own,),
        in_specs=[
            pl.BlockSpec((1, BLOCK, frames), lambda k: (k, 0, 0)),
            pl.BlockSpec((1, size, size), lambda k: (k, 0, 0)),
            pl.BlockSpec((2 * size, 2 * size), lambda k: (0, 0)),
            pl.BlockSpec((2 * size, 2 * size), lambda k: (0, 0)),
        ],
        out_specs=[
            pl.BlockSpec((1, wide, frames * TILE), lambda k: (k, 0, 0)),
            pl.BlockSpec((1, 2 * size, size), lambda k: (k, 0, 0)),
        ],
        out_shape=[
            jax.ShapeDtypeStruct((own, wide, frames * TILE), jnp.bfloat16),
            jax.ShapeDtypeStruct((own, 2 * size, size), jnp.float32),
        ],
        name="prepare",
    )(picked, kernels, forward, backward)

    hbm = pl.BlockSpec(memory_space=pl.ANY)
    half = (frames // 4 * size, 2 * size)
    filtered = pl.pallas_call(
        filter_kernel,
        in_specs=[hbm, hbm, hbm, pl.BlockSpec(memory_space=pltpu.SMEM), hbm],
        out_specs=pl.BlockSpec(memory_space=pltpu.VMEM),
        out_shape=pltpu.VMEM(received.shape, jnp.bfloat16),
        scratch_shapes=[
            pltpu.VMEM((own, tm, space, per_device, rows, size), jnp.bfloat16),
            pltpu.VMEM(time_matrix.shape, jnp.bfloat16),
            pltpu.VMEM(spectra.shape, jnp.float32),
            pltpu.VMEM((2, 2 * size, 2 * size), jnp.bfloat16),
            pltpu.VMEM((frames, space, rows, size), jnp.bfloat16),
            pltpu.VMEM(half, jnp.float32),
            pltpu.VMEM(half, jnp.float32),
            pltpu.SemaphoreType.DMA((own * (space // 2) + own + 2,)),
        ],
        compiler_params=pltpu.CompilerParams(vmem_limit_bytes=VMEM_LIMIT),
        name="filter",
    )(
        received,
        time_matrix,
        spectra,
        gains.reshape(own, 1, 1),
        jnp.stack([forward, backward]).astype(jnp.bfloat16),
    )
    return lax.all_to_all(
        filtered.reshape(latents.shape), AXES, split_axis=0, concat_axis=0, tiled=True
    )


def solution(mesh):
    in_specs = (P(None, "tm", "space", None), P("tm", None), P("tm", None, None), P())
    out_specs = P(None, "tm", "space", None)
    return jax.shard_map(local, mesh=mesh, in_specs=in_specs, out_specs=out_specs, check_vma=False)
```

time: 136 us -> 133 us (0.978)
  Pallas kernels: 16.5 us -> 14.1 us
    pallas_call x1, Pallas kernels: 12.4 us -> 10.2 us  [local(): pl.pallas_call(filter_kernel, in_specs=[hbm, hbm, hbm, pl.BlockSpec(memor...]
where the time goes in v3:
time: 133 us
  blocking collectives  57.1 us (43%)
  waiting for transfers between devices  44.6 us (34%)
  Pallas kernels  14.1 us (11%)
  starting transfers between devices  12 us (9%)
  local copies, waits for them, and re-layouts  3.43 us (3%)
  other arithmetic  1.83 us (1%)
    all_to_all x1, blocking collectives, local(): lax.all_to_all(filtered.reshape(latents.shape), AXES, split_axis=0, conca...  57.1 us
    all_to_all x1, waiting for transfers between devices, local(): lax.all_to_all(latents, AXES, split_axis=0, concat_axis=0, tiled=True)  44.6 us
    all_to_all x1, starting transfers between devices, local(): lax.all_to_all(latents, AXES, split_axis=0, concat_axis=0, tiled=True)  12 us
    pallas_call x1, Pallas kernels, local(): pl.pallas_call(filter_kernel, in_specs=[hbm, hbm, hbm, pl.BlockSpec(memor...  10.2 us
    pallas_call x1, Pallas kernels, local(): pl.pallas_call(prepare_kernel, grid=(own,), in_specs=[pl.BlockSpec((1, BL...  3.93 us
  transfers between devices with their start and end apart: 1, of which 1 were waited for; matrix products, arithmetic and copies ran while one was open for 2% of the time, Pallas kernels for 3%

profile of v3, /device:TPU:1, one launch (start us, length us, event | category | flops | bytes accessed | tf_op | source)
XLA Modules:
  0.0 133.0 jit_solution(3496750963127349355)
XLA Ops:
  0.0 0.0 copy-start
  0.0 0.0 copy-start.1
  0.0 12.0 %all-to-all-start = ((bf16[256,4,16,128]{3,2,1,0:T(8,128)(2,1)}), bf16[256,4,16,128]{3,2,1,0:T(8,128)(2,1)}, u32[]{:S(2)}, u32[]{:S(2)}) async-start(bf16[256,4,16,128]{3,2,1,0:T(8,128)(2,1)} %param.6), calls=%async_computation | async-start | bytes 8388608 | tf_op jit(solution)/shard_map/all_to_all | solution.py:222
  12.0 0.0 copy-done.1
  12.0 0.1 dynamic-slice_bitcast_fusion
  12.1 0.7 copy.8.gain_ref
  12.7 0.7 dynamic-slice_convert_fusion
  13.4 0.0 copy-done
  13.4 0.7 constant_dynamic-slice_fusion.kernel_ref
  14.1 0.2 iota_compare_fusion
  14.3 0.9 select_reduce_fusion.picked_ref
  15.2 3.9 %prepare.1 = (bf16[2,256,512]{2,1,0:T(8,128)(2,1)}, f32[2,256,128]{2,1,0:T(8,128)}) custom-call(bf16[2,32,64]{2,1,0:T(8,128)(2,1)} %select_reduce_fusion.picked_ref, f32[2,128,128]{2,1,0:T(8,128)} %constant_dynamic-slice_fusion.kernel_ref, f32[256,256]{1,0:T(8,128)} %constant.27.clone.forward_ref, f32[256,256]{1,0:T(8,128)} %constant.28.clone.backward_ref), custom_call_target="tpu_custom_call" | custom-call | tf_op jit(solution)/shard_map/prepare/pallas_call | solution.py:240
  19.2 44.6 %all-to-all-done = bf16[256,4,16,128]{3,2,1,0:T(8,128)(2,1)} async-done(((bf16[256,4,16,128]{3,2,1,0:T(8,128)(2,1)}), bf16[256,4,16,128]{3,2,1,0:T(8,128)(2,1)}, u32[]{:S(2)}, u32[]{:S(2)}) %all-to-all-start) | async-done | bytes 4194336 | tf_op jit(solution)/shard_map/all_to_all | solution.py:222
  63.7 10.2 %filter.1 = bf16[16,8,2,4,16,128]{5,4,3,2,1,0:T(8,128)(2,1)S(1)} custom-call(bf16[16,8,2,4,16,128]{5,4,3,2,1,0:T(8,128)(2,1)} %bitcast.x_hbm, bf16[2,256,512]{2,1,0:T(8,128)(2,1)} %get-tuple-element.7.time_hbm, f32[2,256,128]{2,1,0:T(8,128)} %get-tuple-element.8.spec_hbm, f32[2,1,1]{2,1,0:T(1,128)} %copy.8.gain_ref, bf16[2,256,256]{2,1,0:T(8,128)(2,1)} %constant.34.tables_hbm), custom_call_target="tpu_custom_call" | custom-call | tf_op jit(solution)/shard_map/filter/pallas_call | solution.py:262
  73.9 57.1 %all_to_all.10 = bf16[256,4,16,128]{3,2,1,0:T(8,128)(2,1)S(1)} all-to-all(bf16[256,4,16,128]{3,2,1,0:T(8,128)(2,1)S(1)} %bitcast.4), channel_id=1, replica_groups=mesh['tm'=16,'space'=8] {'tm','space'}, dimensions={0} | all-to-all | bytes 8388608 | tf_op jit(solution)/shard_map/all_to_all | solution.py:286
  131.0 2.0 %copy.10 = bf16[256,4,16,128]{3,2,1,0:T(8,128)(2,1)} copy(bf16[256,4,16,128]{3,2,1,0:T(8,128)(2,1)S(1)} %all_to_all.10) | data formatting | bytes 8388608
  (1 shorter events, 0.0 us)
Async XLA Ops:
  0.0 13.4 %copy-start = (f32[16,128,128]{2,1,0:T(8,128)S(1)}, f32[16,128,128]{2,1,0:T(8,128)}, u32[]{:S(2)}) copy-start(f32[16,128,128]{2,1,0:T(8,128)} %param.8) | copy-start | bytes 3145732
  0.0 12.0 %copy-start.1 = (f32[256]{0:T(256)S(1)}, f32[256]{0:T(256)}, u32[]{:S(2)}) copy-start(f32[256]{0:T(256)} %param.9) | copy-start | bytes 3076
  0.0 63.7 %all-to-all-start = ((bf16[256,4,16,128]{3,2,1,0:T(8,128)(2,1)}), bf16[256,4,16,128]{3,2,1,0:T(8,128)(2,1)}, u32[]{:S(2)}, u32[]{:S(2)}) async-start(bf16[256,4,16,128]{3,2,1,0:T(8,128)(2,1)} %param.6), calls=%async_computation | async-start | bytes 8388608 | tf_op jit(solution)/shard_map/all_to_all | solution.py:222

commit v4 on v3

v4 whole, which is shorter than its diff:
```python
import math

import jax
import jax.numpy as jnp
import numpy as np
from jax import lax
from jax.experimental import pallas as pl
from jax.experimental.pallas import tpu as pltpu
from jax.sharding import PartitionSpec as P

AXES = ("tm", "space")
TILE = 8
BLOCK = 32
PARTS = 4
VMEM_LIMIT = 32 * 1024 * 1024


def dft_tables(length):
    positions = np.arange(length)
    angles = (positions[:, None] * positions[None, :] % length) * (2.0 * math.pi / length)
    cos, sin = np.cos(angles), np.sin(angles)
    forward = np.block([[cos, -sin], [sin, cos]])
    return forward.astype(np.float32), forward.T.copy().astype(np.float32)


def gelu_of_scaled(scaled):
    half = scaled * math.sqrt(0.5)
    return half + half * lax.erf(scaled)


def filter_kernel(
    x_ref, taps_ref, exact_ref, kernels_ref, gain_hbm, o_ref,
    tables_ref, rest_ref, time_ref, spec_ref, gain_ref, conv, result_a, result_b, gain_sem,
):
    tm, space, own, per_device, rows, size = x_ref.shape
    frames = tm * per_device
    side_rows = BLOCK * TILE
    blocks = frames // BLOCK
    pieces = space // 2
    pairs = frames // 2
    devices = tm // (2 * PARTS)
    results = (result_a, result_b)
    here = lax.axis_index("space") * own
    group = lax.axis_index("tm") * space * own

    gain_copy = pltpu.make_async_copy(gain_hbm, gain_ref, gain_sem)
    gain_copy.start()

    def dot(a, b):
        return jnp.dot(a, b, preferred_element_type=jnp.float32)

    def two_parts(value):
        high = value.astype(jnp.bfloat16)
        return high, (value - high.astype(jnp.float32)).astype(jnp.bfloat16)

    for table in range(2):
        tables_ref[table], rest_ref[table] = two_parts(exact_ref[table])

    def spread(shape, along):
        wide = lax.broadcasted_iota(jnp.int32, shape, along) // TILE
        return (wide == lax.broadcasted_iota(jnp.int32, shape, 1 - along)).astype(jnp.bfloat16)

    def make_time(k):
        taps = taps_ref[...].astype(jnp.float32)
        row = lax.broadcasted_iota(jnp.int32, taps.shape, 0)
        taps = jnp.sum(jnp.where(row == here + k, taps, 0.0), axis=0, keepdims=True)
        shape = (BLOCK, 2 * frames)
        taps = jnp.broadcast_to(jnp.concatenate([taps, jnp.zeros_like(taps)], axis=1), shape)
        lag = (
            (frames - BLOCK)
            + lax.broadcasted_iota(jnp.int32, shape, 0)
            - lax.broadcasted_iota(jnp.int32, shape, 1)
        )
        picked = jnp.take_along_axis(taps, jnp.maximum(lag, 0), axis=1)
        picked = jnp.where(lag >= 0, picked, 0.0)[:, :frames].astype(jnp.bfloat16)
        tall = dot(spread((side_rows, BLOCK), 0), picked).astype(jnp.bfloat16)
        shape = (side_rows, frames * TILE)
        full = dot(tall, spread((frames, frames * TILE), 1))
        row_of = lax.broadcasted_iota(jnp.int32, shape, 0) % TILE
        col_of = lax.broadcasted_iota(jnp.int32, shape, 1) % TILE
        time_ref[k] = jnp.where(row_of == col_of, full, 0.0).astype(jnp.bfloat16)

    def make_spectra():
        high, rest = two_parts(kernels_ref[pl.ds(here, own)].reshape(own * size, size))
        forward = tables_ref[0, :size]
        half = dot(
            jnp.concatenate([high, rest], axis=1), jnp.concatenate([forward, forward], axis=0)
        ) + dot(high, rest_ref[0, :size])
        stacked = jnp.concatenate(
            [
                jnp.concatenate(
                    [half[k * size : (k + 1) * size, part * size : (part + 1) * size] for part in range(2)],
                    axis=0,
                )
                for k in range(own)
            ],
            axis=1,
        )
        high, rest = two_parts(stacked)
        spectra = dot(tables_ref[1], high) + dot(tables_ref[1], rest) + dot(rest_ref[1], high)
        spectra = spectra * (math.sqrt(0.5) / (size * size))
        for k in range(own):
            spec_ref[k] = spectra[:, k * size : (k + 1) * size]

    def over_time(k, piece):
        sides = [
            x_ref[:, 2 * piece + side, k].reshape(frames, rows, size) for side in range(2)
        ]
        halves = [
            jnp.concatenate(
                [
                    side[:, first : first + TILE].reshape(frames * TILE, size)
                    for side in sides
                ],
                axis=1,
            )
            for first in range(0, rows, TILE)
        ]
        for block in range(blocks):
            summed = jnp.concatenate(
                [
                    dot(
                        time_ref[k, :, (blocks - 1 - block) * side_rows :],
                        half[: (block + 1) * side_rows],
                    ).reshape(BLOCK, TILE, 2 * size)
                    for half in halves
                ],
                axis=1,
            ).astype(jnp.bfloat16)
            for side in range(2):
                conv[block * BLOCK : (block + 1) * BLOCK, 2 * piece + side] = summed[
                    :, :, side * size : (side + 1) * size
                ]

    def stack_rows(value):
        parts = [value[p * size : (p + 1) * size] for p in range(pairs)]
        return jnp.concatenate(
            [
                jnp.concatenate([part[:, :size] for part in parts], axis=1),
                jnp.concatenate([part[:, size:] for part in parts], axis=1),
            ],
            axis=0,
        )

    def stack_cols(value):
        return jnp.concatenate(
            [
                jnp.concatenate(
                    [
                        value[:size, p * size : (p + 1) * size],
                        value[size:, p * size : (p + 1) * size],
                    ],
                    axis=1,
                )
                for p in range(pairs)
            ],
            axis=0,
        )

    def over_space(k):
        forward, backward = tables_ref[0], tables_ref[1]
        images = jnp.concatenate(
            [
                jnp.concatenate(
                    [conv[2 * p + side].reshape(size, size) for side in range(2)], axis=1
                )
                for p in range(pairs)
            ],
            axis=0,
        )
        cols = dot(images, forward).astype(jnp.bfloat16)
        spectrum = dot(backward, stack_rows(cols))
        spec_re = jnp.concatenate([spec_ref[k, :size]] * pairs, axis=1)
        spec_im = jnp.concatenate([spec_ref[k, size:]] * pairs, axis=1)
        re, im = spectrum[:size], spectrum[size:]
        product = jnp.concatenate(
            [re * spec_re - im * spec_im, re * spec_im + im * spec_re], axis=0
        ).astype(jnp.bfloat16)
        restored = stack_cols(dot(forward, product).astype(jnp.bfloat16))
        for half in range(2):
            side = pairs // 2 * size
            results[half][...] = dot(restored[half * side : (half + 1) * side], backward)

    def finish(k, half, part):
        gain = gain_ref[group + here + k] * math.sqrt(0.5)
        for place in range(part * devices * per_device, (part + 1) * devices * per_device):
            device, frame = place // per_device, place % per_device
            p, side = place // 2, place % 2
            filtered = results[half][p * size : (p + 1) * size, side * size : (side + 1) * size]
            source = half * (tm // 2) + device
            latent = x_ref[source, :, k, frame].reshape(size, size).astype(jnp.float32)
            o_ref[source, :, k, frame] = (
                gelu_of_scaled(filtered + gain * latent)
                .astype(jnp.bfloat16)
                .reshape(space, rows, size)
            )

    def time_all(k):
        for piece in range(pieces):
            over_time(k, piece)

    def finish_half(k, half):
        for part in range(PARTS):
            finish(k, half, part)

    make_spectra()
    for k in range(own):
        make_time(k)
    time_all(0)
    gain_copy.wait()
    for k in range(own):
        over_space(k)
        finish_half(k, 0)
        if k + 1 < own:
            time_all(k + 1)
        finish_half(k, 1)


def local(latents, time_taps, space_taps, skip_gain):
    tm, space = lax.axis_size("tm"), lax.axis_size("space")
    channels, per_device, rows, size = latents.shape
    frames = tm * per_device
    own = channels // (tm * space)

    received = lax.all_to_all(latents, AXES, split_axis=0, concat_axis=0, tiled=True)
    received = received.reshape(tm, space, own, per_device, rows, size)

    exact = np.stack(dft_tables(size))
    vmem = pl.BlockSpec(memory_space=pltpu.VMEM)
    half = (frames // 4 * size, 2 * size)
    filtered = pl.pallas_call(
        filter_kernel,
        in_specs=[vmem, vmem, vmem, vmem, pl.BlockSpec(memory_space=pl.ANY)],
        out_specs=vmem,
        out_shape=pltpu.VMEM(received.shape, jnp.bfloat16),
        scratch_shapes=[
            pltpu.VMEM(exact.shape, jnp.bfloat16),
            pltpu.VMEM(exact.shape, jnp.bfloat16),
            pltpu.VMEM((own, BLOCK * TILE, frames * TILE), jnp.bfloat16),
            pltpu.VMEM((own, 2 * size, size), jnp.float32),
            pltpu.SMEM(skip_gain.shape, jnp.float32),
            pltpu.VMEM((frames, space, rows, size), jnp.bfloat16),
            pltpu.VMEM(half, jnp.float32),
            pltpu.VMEM(half, jnp.float32),
            pltpu.SemaphoreType.DMA,
        ],
        compiler_params=pltpu.CompilerParams(vmem_limit_bytes=VMEM_LIMIT),
        name="filter",
    )(
        received,
        time_taps,
        jnp.asarray(exact),
        space_taps,
        skip_gain,
    )
    return lax.all_to_all(
        filtered.reshape(latents.shape), AXES, split_axis=0, concat_axis=0, tiled=True
    )


def solution(mesh):
    in_specs = (P(None, "tm", "space", None), P("tm", None), P("tm", None, None), P())
    out_specs = P(None, "tm", "space", None)
    return jax.shard_map(local, mesh=mesh, in_specs=in_specs, out_specs=out_specs, check_vma=False)
```

time: 133 us -> 132 us (level)
  blocking collectives: 57.1 us -> 121 us
  waiting for transfers between devices: 44.6 us -> 0 us
  starting transfers between devices: 12 us -> 0 us
  Pallas kernels: 14.1 us -> 8.58 us
  other arithmetic: 1.83 us -> 0 us
  local copies, waits for them, and re-layouts: 3.43 us -> 2.03 us
    all_to_all x0 -> x1, blocking collectives: none -> 63.6 us  [local(): lax.all_to_all(latents, AXES, split_axis=0, concat_axis=0, tiled=True)]
    all_to_all x1 -> x0, waiting for transfers between devices: 44.6 us -> none  [local(): lax.all_to_all(latents, AXES, split_axis=0, concat_axis=0, tiled=True)]
    all_to_all x1 -> x0, starting transfers between devices: 12 us -> none  [local(): lax.all_to_all(latents, AXES, split_axis=0, concat_axis=0, tiled=True)]
    pallas_call x2 -> x1, Pallas kernels: 14.1 us -> 8.58 us  [local(): pl.pallas_call(filter_kernel, in_specs=[vmem, vmem, vmem, vmem, pl.BlockS...]
  transfers between devices with their start and end apart: 1 -> 0, of which waited for: 1 -> 0; matrix products, arithmetic and copies ran while one was open for 2% -> 0% of each run, Pallas kernels for 3% -> 0%
where the time goes in v4:
time: 132 us; the launch traced here: 131 us
  blocking collectives  121 us (92%)
  Pallas kernels  8.58 us (6%)
  local copies, waits for them, and re-layouts  2.03 us (2%)
    all_to_all x1, blocking collectives, local(): lax.all_to_all(latents, AXES, split_axis=0, concat_axis=0, tiled=True)  63.6 us
    all_to_all x1, blocking collectives, local(): lax.all_to_all(filtered.reshape(latents.shape), AXES, split_axis=0, conca...  57.1 us
    pallas_call x1, Pallas kernels, local(): pl.pallas_call(filter_kernel, in_specs=[vmem, vmem, vmem, vmem, pl.BlockS...  8.58 us

profile of v4, /device:TPU:1, one launch (start us, length us, event | category | flops | bytes accessed | tf_op | source)
XLA Modules:
  0.0 131.4 jit_solution(9126281828961100169)
XLA Ops:
  0.0 0.0 copy-start.1
  0.0 0.0 copy-start.3
  0.0 0.0 copy-start
  0.0 0.0 copy-start.2
  0.0 63.6 %all_to_all.10 = bf16[256,4,16,128]{3,2,1,0:T(8,128)(2,1)S(1)} all-to-all(bf16[256,4,16,128]{3,2,1,0:T(8,128)(2,1)} %param.5), channel_id=1, replica_groups=mesh['tm'=16,'space'=8] {'tm','space'}, dimensions={0} | all-to-all | bytes 8388608 | tf_op jit(solution)/shard_map/all_to_all | solution.py:225
  63.7 0.0 copy-done.1
  63.7 0.0 copy-done.3
  63.7 0.0 copy-done
  63.7 0.0 copy-done.2
  63.7 8.6 %filter.1 = bf16[16,8,2,4,16,128]{5,4,3,2,1,0:T(8,128)(2,1)S(1)} custom-call(bf16[16,8,2,4,16,128]{5,4,3,2,1,0:T(8,128)(2,1)S(1)} %bitcast.3, bf16[16,64]{1,0:T(8,128)(2,1)S(1)} %copy-done.2, f32[2,256,256]{2,1,0:T(8,128)S(1)} %copy-done.1, f32[16,128,128]{2,1,0:T(8,128)S(1)} %copy-done, f32[256]{0:T(256)S(1)} %copy-done.3), custom_call_target="tpu_custom_call" | custom-call | tf_op jit(solution)/shard_map/filter/pallas_call | solution.py:231
  72.3 57.1 %all_to_all.11 = bf16[256,4,16,128]{3,2,1,0:T(8,128)(2,1)S(1)} all-to-all(bf16[256,4,16,128]{3,2,1,0:T(8,128)(2,1)S(1)} %bitcast.2), channel_id=1, replica_groups=mesh['tm'=16,'space'=8] {'tm','space'}, dimensions={0} | all-to-all | bytes 8388608 | tf_op jit(solution)/shard_map/all_to_all | solution.py:256
  129.4 2.0 %copy.7 = bf16[256,4,16,128]{3,2,1,0:T(8,128)(2,1)} copy(bf16[256,4,16,128]{3,2,1,0:T(8,128)(2,1)S(1)} %all_to_all.11) | data formatting | bytes 8388608
Async XLA Ops:
  0.0 63.7 %copy-start.1 = (f32[2,256,256]{2,1,0:T(8,128)S(1)}, f32[2,256,256]{2,1,0:T(8,128)}, u32[]{:S(2)}) copy-start(f32[2,256,256]{2,1,0:T(8,128)} %constant.2.clone.exact_ref) | copy-start | bytes 1572868
  0.0 63.7 %copy-start.3 = (f32[256]{0:T(256)S(1)}, f32[256]{0:T(256)}, u32[]{:S(2)}) copy-start(f32[256]{0:T(256)} %gain_hbm.1) | copy-start | bytes 3076
  0.0 63.7 %copy-start = (f32[16,128,128]{2,1,0:T(8,128)S(1)}, f32[16,128,128]{2,1,0:T(8,128)}, u32[]{:S(2)}) copy-start(f32[16,128,128]{2,1,0:T(8,128)} %kernels_ref.1) | copy-start | bytes 3145732
  0.0 63.7 %copy-start.2 = (bf16[16,64]{1,0:T(8,128)(2,1)S(1)}, bf16[16,64]{1,0:T(8,128)(2,1)}, u32[]{:S(2)}) copy-start(bf16[16,64]{1,0:T(8,128)(2,1)} %taps_ref.1) | copy-start | bytes 6148

commit v5 on v4

--- a/solution.py
+++ b/solution.py
@@ -37,7 +37,7 @@
     side_rows = BLOCK * TILE
     blocks = frames // BLOCK
     pieces = space // 2
-    pairs = frames // 2
+    pairs = frames // 4
     devices = tm // (2 * PARTS)
     results = (result_a, result_b)
     here = lax.axis_index("space") * own
@@ -56,29 +56,33 @@
     for table in range(2):
         tables_ref[table], rest_ref[table] = two_parts(exact_ref[table])
 
-    def spread(shape, along):
-        wide = lax.broadcasted_iota(jnp.int32, shape, along) // TILE
-        return (wide == lax.broadcasted_iota(jnp.int32, shape, 1 - along)).astype(jnp.bfloat16)
-
     def make_time(k):
         taps = taps_ref[...].astype(jnp.float32)
         row = lax.broadcasted_iota(jnp.int32, taps.shape, 0)
         taps = jnp.sum(jnp.where(row == here + k, taps, 0.0), axis=0, keepdims=True)
-        shape = (BLOCK, 2 * frames)
-        taps = jnp.broadcast_to(jnp.concatenate([taps, jnp.zeros_like(taps)], axis=1), shape)
-        lag = (
-            (frames - BLOCK)
-            + lax.broadcasted_iota(jnp.int32, shape, 0)
-            - lax.broadcasted_iota(jnp.int32, shape, 1)
-        )
-        picked = jnp.take_along_axis(taps, jnp.maximum(lag, 0), axis=1)
-        picked = jnp.where(lag >= 0, picked, 0.0)[:, :frames].astype(jnp.bfloat16)
-        tall = dot(spread((side_rows, BLOCK), 0), picked).astype(jnp.bfloat16)
-        shape = (side_rows, frames * TILE)
-        full = dot(tall, spread((frames, frames * TILE), 1))
-        row_of = lax.broadcasted_iota(jnp.int32, shape, 0) % TILE
-        col_of = lax.broadcasted_iota(jnp.int32, shape, 1) % TILE
-        time_ref[k] = jnp.where(row_of == col_of, full, 0.0).astype(jnp.bfloat16)
+        shape = (BLOCK, frames * TILE)
+        taps = jnp.broadcast_to(jnp.concatenate([taps] * TILE, axis=1), shape)
+        lane = lax.broadcasted_iota(jnp.int32, shape, 1)
+        lag = (frames - BLOCK) + lax.broadcasted_iota(jnp.int32, shape, 0) - lane // TILE
+        parts = []
+        for first in range(0, frames * TILE, size):
+            lanes = slice(first, first + size)
+            parts.append(
+                jnp.take_along_axis(taps[:, lanes], jnp.maximum(lag[:, lanes], 0), axis=1)
+            )
+        picked = jnp.where(lag >= 0, jnp.concatenate(parts, axis=1), 0.0)
+        shape = (TILE, frames * TILE)
+        same_row = lax.broadcasted_iota(jnp.int32, shape, 0) == (
+            lax.broadcasted_iota(jnp.int32, shape, 1) % TILE
+        )
+        for target in range(0, BLOCK, 2):
+            time_ref[k, target * TILE : (target + 2) * TILE] = jnp.concatenate(
+                [
+                    jnp.where(same_row, jnp.broadcast_to(picked[t : t + 1], shape), 0.0)
+                    for t in (target, target + 1)
+                ],
+                axis=0,
+            ).astype(jnp.bfloat16)
 
     def make_spectra():
         high, rest = two_parts(kernels_ref[pl.ds(here, own)].reshape(own * size, size))
@@ -104,12 +108,13 @@
 
     def over_time(k, piece):
         sides = [
-            x_ref[:, 2 * piece + side, k].reshape(frames, rows, size) for side in range(2)
+            x_ref[:, 2 * piece + side, k].reshape(frames, rows, size).astype(jnp.float32)
+            for side in range(2)
         ]
         halves = [
             jnp.concatenate(
                 [
-                    side[:, first : first + TILE].reshape(frames * TILE, size)
+                    side[:, first : first + TILE].reshape(frames * TILE, size).astype(jnp.bfloat16)
                     for side in sides
                 ],
                 axis=1,
@@ -128,7 +133,7 @@
                 axis=1,
             ).astype(jnp.bfloat16)
             for side in range(2):
-                conv[block * BLOCK : (block + 1) * BLOCK, 2 * piece + side] = summed[
+                conv[k, block * BLOCK : (block + 1) * BLOCK, 2 * piece + side] = summed[
                     :, :, side * size : (side + 1) * size
                 ]
 
@@ -157,12 +162,13 @@
             axis=0,
         )
 
-    def over_space(k):
+    def over_space(k, half):
         forward, backward = tables_ref[0], tables_ref[1]
+        first = half * pairs
         images = jnp.concatenate(
             [
                 jnp.concatenate(
-                    [conv[2 * p + side].reshape(size, size) for side in range(2)], axis=1
+                    [conv[k, 2 * (first + p) + side].reshape(size, size) for side in range(2)], axis=1
                 )
                 for p in range(pairs)
             ],
@@ -177,9 +183,7 @@
             [re * spec_re - im * spec_im, re * spec_im + im * spec_re], axis=0
         ).astype(jnp.bfloat16)
         restored = stack_cols(dot(forward, product).astype(jnp.bfloat16))
-        for half in range(2):
-            side = pairs // 2 * size
-            results[half][...] = dot(restored[half * side : (half + 1) * side], backward)
+        results[half][...] = dot(restored, backward)
 
     def finish(k, half, part):
         gain = gain_ref[group + here + k] * math.sqrt(0.5)
@@ -208,12 +212,14 @@
         make_time(k)
     time_all(0)
     gain_copy.wait()
-    for k in range(own):
-        over_space(k)
-        finish_half(k, 0)
-        if k + 1 < own:
-            time_all(k + 1)
-        finish_half(k, 1)
+    for k in range(1, own):
+        time_all(k)
+    halves = [(k, half) for k in range(own) for half in range(2)]
+    over_space(*halves[0])
+    for before, after in zip(halves, halves[1:]):
+        finish_half(*before)
+        over_space(*after)
+    finish_half(*halves[-1])
 
 
 def local(latents, time_taps, space_taps, skip_gain):
@@ -239,7 +245,7 @@
             pltpu.VMEM((own, BLOCK * TILE, frames * TILE), jnp.bfloat16),
             pltpu.VMEM((own, 2 * size, size), jnp.float32),
             pltpu.SMEM(skip_gain.shape, jnp.float32),
-            pltpu.VMEM((frames, space, rows, size), jnp.bfloat16),
+            pltpu.VMEM((own, frames, space, rows, size), jnp.bfloat16),
             pltpu.VMEM(half, jnp.float32),
             pltpu.VMEM(half, jnp.float32),
             pltpu.SemaphoreType.DMA,

time: 132 us -> 131 us (level)
  no operation moved by 1% of the time
where the time goes in v5:
time: 131 us
  blocking collectives  121 us (92%)
  Pallas kernels  7.99 us (6%)
  local copies, waits for them, and re-layouts  2.03 us (2%)
    all_to_all x1, blocking collectives, local(): lax.all_to_all(latents, AXES, split_axis=0, concat_axis=0, tiled=True)  63.6 us
    all_to_all x1, blocking collectives, local(): lax.all_to_all(filtered.reshape(latents.shape), AXES, split_axis=0, conca...  57.1 us
    pallas_call x1, Pallas kernels, local(): pl.pallas_call(filter_kernel, in_specs=[vmem, vmem, vmem, vmem, pl.BlockS...  7.99 us

profile of v5, /device:TPU:1, one launch (start us, length us, event | category | flops | bytes accessed | tf_op | source)
XLA Modules:
  0.0 130.8 jit_solution(3676101048002004924)
XLA Ops:
  0.0 0.0 copy-start.1
  0.0 0.0 copy-start.3
  0.0 0.0 copy-start
  0.0 0.0 copy-start.2
  0.0 63.6 %all_to_all.10 = bf16[256,4,16,128]{3,2,1,0:T(8,128)(2,1)S(1)} all-to-all(bf16[256,4,16,128]{3,2,1,0:T(8,128)(2,1)} %param.5), channel_id=1, replica_groups=mesh['tm'=16,'space'=8] {'tm','space'}, dimensions={0} | all-to-all | bytes 8388608 | tf_op jit(solution)/shard_map/all_to_all | solution.py:231
  63.7 0.0 copy-done.1
  63.7 0.0 copy-done.3
  63.7 0.0 copy-done
  63.7 0.0 copy-done.2
  63.7 8.0 %filter.1 = bf16[16,8,2,4,16,128]{5,4,3,2,1,0:T(8,128)(2,1)S(1)} custom-call(bf16[16,8,2,4,16,128]{5,4,3,2,1,0:T(8,128)(2,1)S(1)} %bitcast.3, bf16[16,64]{1,0:T(8,128)(2,1)S(1)} %copy-done.2, f32[2,256,256]{2,1,0:T(8,128)S(1)} %copy-done.1, f32[16,128,128]{2,1,0:T(8,128)S(1)} %copy-done, f32[256]{0:T(256)S(1)} %copy-done.3), custom_call_target="tpu_custom_call" | custom-call | tf_op jit(solution)/shard_map/filter/pallas_call | solution.py:237
  71.7 57.1 %all_to_all.11 = bf16[256,4,16,128]{3,2,1,0:T(8,128)(2,1)S(1)} all-to-all(bf16[256,4,16,128]{3,2,1,0:T(8,128)(2,1)S(1)} %bitcast.2), channel_id=1, replica_groups=mesh['tm'=16,'space'=8] {'tm','space'}, dimensions={0} | all-to-all | bytes 8388608 | tf_op jit(solution)/shard_map/all_to_all | solution.py:262
  128.8 2.0 %copy.7 = bf16[256,4,16,128]{3,2,1,0:T(8,128)(2,1)} copy(bf16[256,4,16,128]{3,2,1,0:T(8,128)(2,1)S(1)} %all_to_all.11) | data formatting | bytes 8388608
Async XLA Ops:
  0.0 63.7 %copy-start.1 = (f32[2,256,256]{2,1,0:T(8,128)S(1)}, f32[2,256,256]{2,1,0:T(8,128)}, u32[]{:S(2)}) copy-start(f32[2,256,256]{2,1,0:T(8,128)} %constant.2.clone.exact_ref) | copy-start | bytes 1572868
  0.0 63.7 %copy-start.3 = (f32[256]{0:T(256)S(1)}, f32[256]{0:T(256)}, u32[]{:S(2)}) copy-start(f32[256]{0:T(256)} %gain_hbm.1) | copy-start | bytes 3076
  0.0 63.7 %copy-start = (f32[16,128,128]{2,1,0:T(8,128)S(1)}, f32[16,128,128]{2,1,0:T(8,128)}, u32[]{:S(2)}) copy-start(f32[16,128,128]{2,1,0:T(8,128)} %kernels_ref.1) | copy-start | bytes 3145732
  0.0 63.7 %copy-start.2 = (bf16[16,64]{1,0:T(8,128)(2,1)S(1)}, bf16[16,64]{1,0:T(8,128)(2,1)}, u32[]{:S(2)}) copy-start(bf16[16,64]{1,0:T(8,128)(2,1)} %taps_ref.1) | copy-start | bytes 6148

commit v6 on v5

--- a/solution.py
+++ b/solution.py
@@ -12,13 +12,14 @@
 TILE = 8
 BLOCK = 32
 PARTS = 4
+TABLE_SCALE = 1.62475
 VMEM_LIMIT = 32 * 1024 * 1024
 
 
 def dft_tables(length):
     positions = np.arange(length)
     angles = (positions[:, None] * positions[None, :] % length) * (2.0 * math.pi / length)
-    cos, sin = np.cos(angles), np.sin(angles)
+    cos, sin = TABLE_SCALE * np.cos(angles), TABLE_SCALE * np.sin(angles)
     forward = np.block([[cos, -sin], [sin, cos]])
     return forward.astype(np.float32), forward.T.copy().astype(np.float32)
 
@@ -102,7 +103,7 @@
         )
         high, rest = two_parts(stacked)
         spectra = dot(tables_ref[1], high) + dot(tables_ref[1], rest) + dot(rest_ref[1], high)
-        spectra = spectra * (math.sqrt(0.5) / (size * size))
+        spectra = spectra * (math.sqrt(0.5) / (size * size * TABLE_SCALE**6))
         for k in range(own):
             spec_ref[k] = spectra[:, k * size : (k + 1) * size]
 

time: 131 us -> 131 us (level)
  no operation moved by 1% of the time
where the time goes in v6:
time: 131 us
  blocking collectives  121 us (92%)
  Pallas kernels  7.99 us (6%)
  local copies, waits for them, and re-layouts  2.03 us (2%)
    all_to_all x1, blocking collectives, local(): lax.all_to_all(latents, AXES, split_axis=0, concat_axis=0, tiled=True)  63.6 us
    all_to_all x1, blocking collectives, local(): lax.all_to_all(filtered.reshape(latents.shape), AXES, split_axis=0, conca...  57.1 us
    pallas_call x1, Pallas kernels, local(): pl.pallas_call(filter_kernel, in_specs=[vmem, vmem, vmem, vmem, pl.BlockS...  7.99 us

profile of v6, /device:TPU:1, one launch (start us, length us, event | category | flops | bytes accessed | tf_op | source)
XLA Modules:
  0.0 130.8 jit_solution(13771121576148560848)
XLA Ops:
  0.0 0.0 copy-start.1
  0.0 0.0 copy-start.3
  0.0 0.0 copy-start
  0.0 0.0 copy-start.2
  0.0 63.6 %all_to_all.10 = bf16[256,4,16,128]{3,2,1,0:T(8,128)(2,1)S(1)} all-to-all(bf16[256,4,16,128]{3,2,1,0:T(8,128)(2,1)} %param.5), channel_id=1, replica_groups=mesh['tm'=16,'space'=8] {'tm','space'}, dimensions={0} | all-to-all | bytes 8388608 | tf_op jit(solution)/shard_map/all_to_all | solution.py:232
  63.7 0.0 copy-done.1
  63.7 0.0 copy-done.3
  63.7 0.0 copy-done
  63.7 0.0 copy-done.2
  63.7 8.0 %filter.1 = bf16[16,8,2,4,16,128]{5,4,3,2,1,0:T(8,128)(2,1)S(1)} custom-call(bf16[16,8,2,4,16,128]{5,4,3,2,1,0:T(8,128)(2,1)S(1)} %bitcast.3, bf16[16,64]{1,0:T(8,128)(2,1)S(1)} %copy-done.2, f32[2,256,256]{2,1,0:T(8,128)S(1)} %copy-done.1, f32[16,128,128]{2,1,0:T(8,128)S(1)} %copy-done, f32[256]{0:T(256)S(1)} %copy-done.3), custom_call_target="tpu_custom_call" | custom-call | tf_op jit(solution)/shard_map/filter/pallas_call | solution.py:238
  71.7 57.1 %all_to_all.11 = bf16[256,4,16,128]{3,2,1,0:T(8,128)(2,1)S(1)} all-to-all(bf16[256,4,16,128]{3,2,1,0:T(8,128)(2,1)S(1)} %bitcast.2), channel_id=1, replica_groups=mesh['tm'=16,'space'=8] {'tm','space'}, dimensions={0} | all-to-all | bytes 8388608 | tf_op jit(solution)/shard_map/all_to_all | solution.py:263
  128.8 2.0 %copy.7 = bf16[256,4,16,128]{3,2,1,0:T(8,128)(2,1)} copy(bf16[256,4,16,128]{3,2,1,0:T(8,128)(2,1)S(1)} %all_to_all.11) | data formatting | bytes 8388608
Async XLA Ops:
  0.0 63.7 %copy-start.1 = (f32[2,256,256]{2,1,0:T(8,128)S(1)}, f32[2,256,256]{2,1,0:T(8,128)}, u32[]{:S(2)}) copy-start(f32[2,256,256]{2,1,0:T(8,128)} %constant.2.clone.exact_ref) | copy-start | bytes 1572868
  0.0 63.7 %copy-start.3 = (f32[256]{0:T(256)S(1)}, f32[256]{0:T(256)}, u32[]{:S(2)}) copy-start(f32[256]{0:T(256)} %gain_hbm.1) | copy-start | bytes 3076
  0.0 63.7 %copy-start = (f32[16,128,128]{2,1,0:T(8,128)S(1)}, f32[16,128,128]{2,1,0:T(8,128)}, u32[]{:S(2)}) copy-start(f32[16,128,128]{2,1,0:T(8,128)} %kernels_ref.1) | copy-start | bytes 3145732
  0.0 63.7 %copy-start.2 = (bf16[16,64]{1,0:T(8,128)(2,1)S(1)}, bf16[16,64]{1,0:T(8,128)(2,1)}, u32[]{:S(2)}) copy-start(bf16[16,64]{1,0:T(8,128)(2,1)} %taps_ref.1) | copy-start | bytes 6148

commit v7 on v6

--- a/solution.py
+++ b/solution.py
@@ -25,7 +25,8 @@
 
 
 def gelu_of_scaled(scaled):
-    half = scaled * math.sqrt(0.5)
+    scaled = scaled.astype(jnp.bfloat16)
+    half = scaled * jnp.bfloat16(math.sqrt(0.5))
     return half + half * lax.erf(scaled)
 
 

time: 131 us -> 131 us (level)
  no operation moved by 1% of the time
where the time goes in v7:
time: 131 us
  blocking collectives  121 us (92%)
  Pallas kernels  7.94 us (6%)
  local copies, waits for them, and re-layouts  2.03 us (2%)
    all_to_all x1, blocking collectives, local(): lax.all_to_all(latents, AXES, split_axis=0, concat_axis=0, tiled=True)  63.6 us
    all_to_all x1, blocking collectives, local(): lax.all_to_all(filtered.reshape(latents.shape), AXES, split_axis=0, conca...  57.1 us
    pallas_call x1, Pallas kernels, local(): pl.pallas_call(filter_kernel, in_specs=[vmem, vmem, vmem, vmem, pl.BlockS...  7.94 us

profile of v7, /device:TPU:1, one launch (start us, length us, event | category | flops | bytes accessed | tf_op | source)
XLA Modules:
  0.0 130.8 jit_solution(4302276248923788926)
XLA Ops:
  0.0 0.0 copy-start.1
  0.0 0.0 copy-start.3
  0.0 0.0 copy-start
  0.0 0.0 copy-start.2
  0.0 63.6 %all_to_all.10 = bf16[256,4,16,128]{3,2,1,0:T(8,128)(2,1)S(1)} all-to-all(bf16[256,4,16,128]{3,2,1,0:T(8,128)(2,1)} %param.5), channel_id=1, replica_groups=mesh['tm'=16,'space'=8] {'tm','space'}, dimensions={0} | all-to-all | bytes 8388608 | tf_op jit(solution)/shard_map/all_to_all | solution.py:233
  63.7 0.0 copy-done.1
  63.7 0.0 copy-done.3
  63.7 0.0 copy-done
  63.7 0.0 copy-done.2
  63.7 7.9 %filter.1 = bf16[16,8,2,4,16,128]{5,4,3,2,1,0:T(8,128)(2,1)S(1)} custom-call(bf16[16,8,2,4,16,128]{5,4,3,2,1,0:T(8,128)(2,1)S(1)} %bitcast.3, bf16[16,64]{1,0:T(8,128)(2,1)S(1)} %copy-done.2, f32[2,256,256]{2,1,0:T(8,128)S(1)} %copy-done.1, f32[16,128,128]{2,1,0:T(8,128)S(1)} %copy-done, f32[256]{0:T(256)S(1)} %copy-done.3), custom_call_target="tpu_custom_call" | custom-call | tf_op jit(solution)/shard_map/filter/pallas_call | solution.py:239
  71.6 57.1 %all_to_all.11 = bf16[256,4,16,128]{3,2,1,0:T(8,128)(2,1)S(1)} all-to-all(bf16[256,4,16,128]{3,2,1,0:T(8,128)(2,1)S(1)} %bitcast.2), channel_id=1, replica_groups=mesh['tm'=16,'space'=8] {'tm','space'}, dimensions={0} | all-to-all | bytes 8388608 | tf_op jit(solution)/shard_map/all_to_all | solution.py:264
  128.7 2.0 %copy.7 = bf16[256,4,16,128]{3,2,1,0:T(8,128)(2,1)} copy(bf16[256,4,16,128]{3,2,1,0:T(8,128)(2,1)S(1)} %all_to_all.11) | data formatting | bytes 8388608
Async XLA Ops:
  0.0 63.7 %copy-start.1 = (f32[2,256,256]{2,1,0:T(8,128)S(1)}, f32[2,256,256]{2,1,0:T(8,128)}, u32[]{:S(2)}) copy-start(f32[2,256,256]{2,1,0:T(8,128)} %constant.2.clone.exact_ref) | copy-start | bytes 1572868
  0.0 63.7 %copy-start.3 = (f32[256]{0:T(256)S(1)}, f32[256]{0:T(256)}, u32[]{:S(2)}) copy-start(f32[256]{0:T(256)} %gain_hbm.1) | copy-start | bytes 3076
  0.0 63.7 %copy-start = (f32[16,128,128]{2,1,0:T(8,128)S(1)}, f32[16,128,128]{2,1,0:T(8,128)}, u32[]{:S(2)}) copy-start(f32[16,128,128]{2,1,0:T(8,128)} %kernels_ref.1) | copy-start | bytes 3145732
  0.0 63.7 %copy-start.2 = (bf16[16,64]{1,0:T(8,128)(2,1)S(1)}, bf16[16,64]{1,0:T(8,128)(2,1)}, u32[]{:S(2)}) copy-start(bf16[16,64]{1,0:T(8,128)(2,1)} %taps_ref.1) | copy-start | bytes 6148
